TPU v7x, 512 devices: a whole 4x4x16 slice. The times are simulated.
512 devices in a mesh: dp: 128 (over x, z, core), mp: 4 (over y).
Axes of the slice: x: 4, y: 4, z: 16, core: 2. Of those that a mesh axis runs over, the one named last changes fastest.
Arguments:
- q_hidden: bfloat16 [8192, 4096], P('dp', 'mp'), may hold values from -0.09375 to 0.09375
- p_hidden: bfloat16 [8192, 4096], P('dp', 'mp'), may hold values from -0.09375 to 0.09375
- proj: bfloat16 [4096, 4096], P('dp', 'mp'), may hold values from -0.25 to 0.25
- positives: int32 [8192], P('dp'), may hold values from 0 to 8191, as said below
- negatives: int32 [8192, 16], P('dp'), may hold values from 0 to 8191, as said below
Outputs:
- grad_q_hidden: bfloat16 [8192, 4096], P('dp', 'mp')
- grad_p_hidden: bfloat16 [8192, 4096], P('dp', 'mp')
- query_loss: float32 [8192], P('dp')
Inputs may be any that keep to these rules, and one draw needn't show every extreme that they name: `positives`: the positive of a query is a passage held by the same index of dp as the query (passages i * 64 to (i + 1) * 64 - 1 on index i), and each such passage is the positive of exactly one of that device's queries. Passage p is held by index p // 64 of dp. The 1024 negatives of one index's queries name, counting repeats, at most 12 passages held by any one index; one index is named exactly 12 times by the queries of every index. Negatives are mined per device from a shared pool: for each holder, a device's queries draw from the same four passages of that holder. A query's negatives are four runs of four consecutive entries; each run names those four distinct passages of one holder, and all runs that one index's queries direct to one holder name them in the same order. A negative may repeat or equal the positive.
All inputs are finite; a program needn't handle non-finite values.
Results may differ from a plain program's by a relative error of at most 0.019.
Values may be sent and summed in bfloat16 or wider, within the bound.
A program may use at most 128 MiB of HBM per device.

v0:
```python
import jax
import jax.numpy as jnp
from jax import lax
from jax.sharding import PartitionSpec as P

SCALE = 20.0
EPS = 1e-06


def unit_backward(grad_unit, unit_exact, radius, inner):
    return ((grad_unit - unit_exact * inner[:, None]) / radius[:, None]).astype(jnp.bfloat16)


def project_back(grad_emb, w_cols):
    return lax.dot_general(
        grad_emb, w_cols, (((1,), (1,)), ((), ())), preferred_element_type=jnp.float32
    )


def body(q_hidden, p_hidden, proj, positives, negatives):
    row_count = q_hidden.shape[0]
    feat_width = q_hidden.shape[1]
    peer_count = lax.axis_size("dp")
    q_full, p_full = (
        lax.all_gather(q_hidden, "mp", axis=1, tiled=True),
        lax.all_gather(p_hidden, "mp", axis=1, tiled=True),
    )
    stacked = jnp.concatenate([q_full, p_full], axis=0)
    w_cols = lax.all_gather(proj, "dp", axis=0, tiled=True)
    embedded = jnp.dot(stacked, w_cols, preferred_element_type=jnp.float32)
    emb_wide = embedded.astype(jnp.bfloat16).astype(jnp.float32)
    squares = jnp.sum(emb_wide * emb_wide, axis=1)
    q_sq, p_sq = lax.psum((squares[:row_count], squares[row_count:]), "mp")
    q_radius = jnp.sqrt(q_sq + EPS)
    p_radius = jnp.sqrt(p_sq + EPS)
    q_exact = emb_wide[:row_count] / q_radius[:, None]
    p_exact = emb_wide[row_count:] / p_radius[:, None]
    q_unit = q_exact.astype(jnp.bfloat16)
    p_unit = p_exact.astype(jnp.bfloat16)
    neg_count = negatives.shape[1]
    flat_ids = negatives.reshape(-1)
    slot_count = flat_ids.shape[0]
    slot_cap = 3 * (slot_count // peer_count) // 2
    owners = flat_ids // row_count
    local_ids = flat_ids % row_count
    owner_hits = (owners[:, None] == jnp.arange(peer_count, dtype=jnp.int32)[None, :]).astype(
        jnp.int32
    )
    slot_rank = jnp.sum(jnp.cumsum(owner_hits, axis=0) * owner_hits, axis=1) - 1
    slot_place = owners * slot_cap + slot_rank
    requests = (
        jnp.zeros((peer_count * slot_cap,), jnp.int32)
        .at[slot_place]
        .set(local_ids)
        .reshape(peer_count, slot_cap)
    )
    wanted = lax.all_to_all(requests, "dp", split_axis=0, concat_axis=0, tiled=True)
    answers = p_unit[wanted.reshape(-1)].reshape(peer_count, slot_cap, feat_width)
    returned = lax.all_to_all(answers, "dp", split_axis=0, concat_axis=0, tiled=True)
    fetched = returned.reshape(peer_count * slot_cap, feat_width)[slot_place]
    fetched = fetched.reshape(row_count, neg_count, feat_width)
    own_pos = positives % row_count
    pos_rows = p_unit[own_pos]
    score_pos = jnp.einsum("qf,qf->q", q_unit, pos_rows, preferred_element_type=jnp.float32)
    score_neg = jnp.einsum("qf,qkf->qk", q_unit, fetched, preferred_element_type=jnp.float32)
    score_parts = jnp.concatenate([score_pos[:, None], score_neg], axis=1)
    scores = SCALE * lax.psum(score_parts, "mp")
    exp_scores = jnp.exp(scores)
    denominator = jnp.sum(exp_scores, axis=1)
    probs = exp_scores / denominator[:, None]
    query_loss = jnp.log(denominator) - scores[:, 0]
    target = (jnp.arange(neg_count + 1) == 0).astype(jnp.float32)
    coef = SCALE * (probs - target[None, :])
    q_wide = q_unit.astype(jnp.float32)
    g_qunit = coef[:, 0:1] * pos_rows.astype(jnp.float32) + jnp.einsum(
        "qk,qkf->qf", coef[:, 1:], fetched.astype(jnp.float32), precision=lax.Precision.HIGHEST
    )
    pos_term = (coef[:, 0:1] * q_wide).astype(jnp.bfloat16)
    neg_term = (coef[:, 1:, None] * q_wide[:, None, :]).astype(jnp.bfloat16)
    outgoing = (
        jnp.zeros((peer_count * slot_cap, feat_width), jnp.bfloat16)
        .at[slot_place]
        .set(neg_term.reshape(slot_count, feat_width))
        .reshape(peer_count, slot_cap, feat_width)
    )
    incoming = lax.all_to_all(outgoing, "dp", split_axis=0, concat_axis=0, tiled=True).reshape(
        peer_count * slot_cap, feat_width
    )
    row_ids = jnp.arange(row_count, dtype=jnp.int32)
    hit_table = (wanted.reshape(-1)[:, None] == row_ids[None, :]).astype(jnp.bfloat16)
    pos_table = (own_pos[:, None] == row_ids[None, :]).astype(jnp.bfloat16)
    g_punit = jnp.einsum(
        "sr,sf->rf", hit_table, incoming, preferred_element_type=jnp.float32
    ) + jnp.einsum("sr,sf->rf", pos_table, pos_term, preferred_element_type=jnp.float32)
    q_inner_part = jnp.sum(q_exact * g_qunit, axis=1)
    p_inner_part = jnp.sum(p_exact * g_punit, axis=1)
    q_inner, p_inner = lax.psum((q_inner_part, p_inner_part), "mp")
    g_emb = jnp.concatenate(
        [
            unit_backward(g_qunit, q_exact, q_radius, q_inner),
            unit_backward(g_punit, p_exact, p_radius, p_inner),
        ],
        axis=0,
    )
    grads = lax.psum_scatter(
        project_back(g_emb, w_cols).astype(jnp.bfloat16), "mp", scatter_dimension=1, tiled=True
    )
    grad_q_hidden = grads[:row_count]
    grad_p_hidden = grads[row_count:]
    return (grad_q_hidden, grad_p_hidden, query_loss)


def solution(mesh):
    placed = (P("dp", "mp"), P("dp", "mp"), P("dp", "mp"), P("dp"), P("dp", None))
    return jax.shard_map(
        body,
        mesh=mesh,
        in_specs=placed,
        out_specs=(P("dp", "mp"), P("dp", "mp"), P("dp")),
        check_vma=False,
    )
```

profile of v0, /device:TPU:1, one launch (start us, length us, event | category | flops | bytes accessed | tf_op | source)
XLA Modules:
  0.0 678.6 jit_solution(11286875059463351698)
XLA Ops:
  7.2 0.7 all-gather.2.cloned.1.call-update
  7.9 0.8 copy.14
  9.1 0.2 fusion.9
  9.5 0.4 fusion.8
  9.9 4.3 scatter_custom_fusion
  14.2 0.7 all_to_all.12
  15.0 20.4 %all-to-all-start = ((s32[128,1,12]{2,1,0:T(1,128)}), s32[128,1,12]{2,1,0:T(1,128)S(1)}, u32[]{:S(2)}, u32[]{:S(2)}) async-start(s32[128,1,12]{2,1,0:T(1,128)} %bitcast.7), calls=%async_computation | async-start | bytes 131072 | tf_op jit(solution)/shard_map/all_to_all | solution.py:57
  35.4 12.0 %all_gather.9 = bf16[64,4096]{1,0:T(8,128)(2,1)S(1)} all-gather(bf16[64,1024]{1,0:T(8,128)(2,1)S(1)} %copy-done.8), channel_id=1, replica_groups=mesh['dp'=128,'mp'=4] {'mp'}, dimensions={1}, use_global_device_ids=true | all-gather | bytes 655360 | tf_op jit(solution)/shard_map/all_gather | solution.py:25
  47.4 10.7 %all_gather.10 = bf16[64,4096]{1,0:T(8,128)(2,1)S(1)} all-gather(bf16[64,1024]{1,0:T(8,128)(2,1)S(1)} %copy-done.9), channel_id=1, replica_groups=mesh['dp'=128,'mp'=4] {'mp'}, dimensions={1}, use_global_device_ids=true | all-gather | bytes 655360 | tf_op jit(solution)/shard_map/all_gather | solution.py:26
  58.1 0.5 broadcast.243
  58.6 0.8 reduce.9
  59.5 0.1 reshape.210
  59.6 104.3 %all-gather.2.cloned.1.call-done = bf16[4096,1024]{1,0:T(8,128)(2,1)} async-done(((bf16[32,1024]{1,0:T(8,128)(2,1)}), bf16[4096,1024]{1,0:T(8,128)(2,1)}) %all-gather.2.cloned.1.call-update) | async-done | bytes 8388624 | tf_op jit(solution)/shard_map/all_gather | solution.py:29
  164.0 4.7 multiply_reduce_fusion
  168.8 8.4 %all-reduce.1 = (f32[64]{0:T(128)S(1)}, f32[64]{0:T(128)S(1)}) all-reduce(f32[64]{0:T(128)S(1)} %get-tuple-element.24, f32[64]{0:T(128)S(1)} %get-tuple-element.23), channel_id=1, replica_groups=mesh['dp'=128,'mp'=4] {'mp'}, use_global_device_ids=true, to_apply=%region_1.0 | all-reduce | flops 128 | bytes 1024 | tf_op jit(solution)/shard_map/psum | solution.py:33
  177.3 5.1 gather_fusion.1
  182.4 2.7 reshape.211
  185.1 12.6 %all-to-all-start.1 = ((bf16[128,12,1024]{2,1,0:T(8,128)(2,1)}), bf16[128,12,1024]{2,1,0:T(8,128)(2,1)}, u32[]{:S(2)}, u32[]{:S(2)}) async-start(bf16[128,12,1024]{2,1,0:T(8,128)(2,1)} %reshape.211), calls=%async_computation.1 | async-start | bytes 8388608 | tf_op jit(solution)/shard_map/all_to_all | solution.py:59
  197.7 0.5 compare_convert_fusion
  198.2 0.6 compare_select_fusion.5
  198.8 0.7 gather_fusion
  199.6 0.2 fusion.12
  199.8 0.6 copy-done.6
  200.4 182.5 %all-to-all-done.1 = bf16[128,12,1024]{2,1,0:T(8,128)(2,1)} async-done(((bf16[128,12,1024]{2,1,0:T(8,128)(2,1)}), bf16[128,12,1024]{2,1,0:T(8,128)(2,1)}, u32[]{:S(2)}, u32[]{:S(2)}) %all-to-all-start.1) | async-done | bytes 3145760 | tf_op jit(solution)/shard_map/all_to_all | solution.py:59
  383.0 4.7 reshape.212
  387.7 5.4 gather_fusion.2
  393.1 2.5 fusion.17
  395.7 11.0 %psum.37 = f32[64,17]{0,1:T(8,128)S(1)} all-reduce(f32[64,17]{0,1:T(8,128)S(1)} %pad_maximum_fusion), channel_id=1, replica_groups=mesh['dp'=128,'mp'=4] {'mp'}, use_global_device_ids=true, to_apply=%region_7.8 | all-reduce | flops 1088 | bytes 8704 | tf_op jit(solution)/shard_map/psum | solution.py:67
  406.7 0.6 broadcast_multiply_fusion
  407.3 0.7 subtract_multiply_fusion
  408.0 0.6 slice_bitcast_fusion.3
  408.8 1.7 fusion
  410.4 7.0 %scatter_custom_fusion.1 = bf16[1536,1024]{1,0:T(8,128)(2,1)S(1)} fusion(s32[1024]{0:T(1024)S(1)} %bitcast.49, bf16[1024,1024]{1,0:T(8,128)(2,1)} %fusion, bf16[]{:T(256)} %constant.60.clone.1), kind=kCustom, calls=%fused_computation.8 | custom fusion | bytes 3146240 | tf_op jit(solution)/shard_map/scatter | solution.py:83
  417.5 2.7 reshape.214
  420.2 16.2 %all-to-all-start.2 = ((bf16[128,12,1024]{2,1,0:T(8,128)(2,1)}), bf16[128,12,1024]{2,1,0:T(8,128)(2,1)}, u32[]{:S(2)}, u32[]{:S(2)}) async-start(bf16[128,12,1024]{2,1,0:T(8,128)(2,1)} %reshape.214), calls=%async_computation.2 | async-start | bytes 8388608 | tf_op jit(solution)/shard_map/all_to_all | solution.py:86
  436.4 0.7 eq.67
  437.2 0.5 slice_bitcast_fusion.2
  437.7 1.0 fusion.39
  438.7 182.9 %all-to-all-done.2 = bf16[128,12,1024]{2,1,0:T(8,128)(2,1)} async-done(((bf16[128,12,1024]{2,1,0:T(8,128)(2,1)}), bf16[128,12,1024]{2,1,0:T(8,128)(2,1)}, u32[]{:S(2)}, u32[]{:S(2)}) %all-to-all-start.2) | async-done | bytes 3145760 | tf_op jit(solution)/shard_map/all_to_all | solution.py:86
  621.7 4.7 reshape.215
  626.4 0.9 fusion.7
  627.5 0.4 multiply_reduce_fusion.2
  627.9 6.8 all-reduce
  634.6 1.3 divide_convert_fusion.1
  635.9 7.3 %convolution_convert_fusion = bf16[128,4096]{1,0:T(8,128)(2,1)} fusion(bf16[4096,1024]{1,0:T(8,128)(2,1)} %all-gather.2.cloned.1.call-done, bf16[64,1024]{1,0:T(8,128)(2,1)S(1)} %get-tuple-element.14, bf16[64,1024]{1,0:T(8,128)(2,1)S(1)} %get-tuple-element.13), kind=kOutput, calls=%fused_computation.5 | convolution fusion | flops 1074790400 | bytes 9699328 | tf_op jit(solution)/shard_map/dot_general | solution.py:15
  643.3 1.2 fusion.31
  644.5 25.6 %reduce-scatter.2.cloned.1.call-done = bf16[128,1024]{1,0:T(8,128)(2,1)} async-done(((bf16[128,4096]{1,0:T(8,128)(2,1)}), bf16[128,1024]{1,0:T(8,128)(2,1)}) %reduce-scatter.2.cloned.1.call-update) | async-done | bytes 262160 | tf_op jit(solution)/shard_map/reduce_scatter | solution.py:105
  670.1 1.7 fusion.37
  (71 shorter events, 1.3 us)
Async XLA Ops:
  7.2 28.2 %copy-start.8 = (bf16[64,1024]{1,0:T(8,128)(2,1)S(1)}, bf16[64,1024]{1,0:T(8,128)(2,1)}, u32[]{:S(2)}) copy-start(bf16[64,1024]{1,0:T(8,128)(2,1)} %param.5) | copy-start | bytes 393220
  7.2 40.2 %copy-start.9 = (bf16[64,1024]{1,0:T(8,128)(2,1)S(1)}, bf16[64,1024]{1,0:T(8,128)(2,1)}, u32[]{:S(2)}) copy-start(bf16[64,1024]{1,0:T(8,128)(2,1)} %param.6) | copy-start | bytes 393220
  7.2 156.8 %all-gather.2.cloned.1.call-start = ((), (), s32[]{:S(2)}) async-start(), calls=%async_computation.4 | async-start | bytes 8454144 | tf_op jit(solution)/shard_map/all_gather | solution.py:29
  15.0 43.2 %all-to-all-start = ((s32[128,1,12]{2,1,0:T(1,128)}), s32[128,1,12]{2,1,0:T(1,128)S(1)}, u32[]{:S(2)}, u32[]{:S(2)}) async-start(s32[128,1,12]{2,1,0:T(1,128)} %bitcast.7), calls=%async_computation | async-start | bytes 131072 | tf_op jit(solution)/shard_map/all_to_all | solution.py:57
  58.1 110.6 %copy-start.4 = (s32[128,1,12]{2,1,0:T(1,128)}, s32[128,1,12]{2,1,0:T(1,128)S(1)}, u32[]{:S(2)}) copy-start(s32[128,1,12]{2,1,0:T(1,128)S(1)} %all-to-all-done) | copy-start | bytes 18436
  168.7 8.5 %copy-start.1 = (f32[128,1024]{1,0:T(8,128)}, f32[128,1024]{1,0:T(8,128)S(1)}, u32[]{:S(2)}) copy-start(f32[128,1024]{1,0:T(8,128)S(1)} %get-tuple-element.26) | copy-start | bytes 1572868
  177.2 5.2 copy-start.12
  177.2 22.4 %copy-start.14 = (f32[64]{0:T(128)}, f32[64]{0:T(128)S(1)}, u32[]{:S(2)}) copy-start(f32[64]{0:T(128)S(1)} %get-tuple-element.29) | copy-start | bytes 772
  185.1 13.1 %copy-start.19 = (s32[64]{0:T(128)S(1)}, s32[64]{0:T(128)}, u32[]{:S(2)}) copy-start(s32[64]{0:T(128)} %param.8) | copy-start | bytes 772
  185.1 14.4 %copy-start.2 = (f32[128,1024]{1,0:T(8,128)S(1)}, f32[128,1024]{1,0:T(8,128)}, u32[]{:S(2)}) copy-start(f32[128,1024]{1,0:T(8,128)} %copy-done.1) | copy-start | bytes 1572868
  185.1 197.9 %all-to-all-start.1 = ((bf16[128,12,1024]{2,1,0:T(8,128)(2,1)}), bf16[128,12,1024]{2,1,0:T(8,128)(2,1)}, u32[]{:S(2)}, u32[]{:S(2)}) async-start(bf16[128,12,1024]{2,1,0:T(8,128)(2,1)} %reshape.211), calls=%async_computation.1 | async-start | bytes 8388608 | tf_op jit(solution)/shard_map/all_to_all | solution.py:59
  199.8 0.7 copy-start.6
  407.3 1.3 copy-start.16
  420.2 16.3 %copy-start.5 = (s32[128,1,12]{2,1,0:T(1,128)S(1)}, s32[128,1,12]{2,1,0:T(1,128)}, u32[]{:S(2)}) copy-start(s32[128,1,12]{2,1,0:T(1,128)} %copy-done.4) | copy-start | bytes 18436
  420.2 17.0 %copy-start.11 = (f32[64,16,1]{0,1,2:T(8,128)S(1)}, f32[64,16,1]{0,1,2:T(8,128)}, u32[]{:S(2)}) copy-start(f32[64,16,1]{0,1,2:T(8,128)} %get-tuple-element.19) | copy-start | bytes 12292
  420.2 17.6 %copy-start = (bf16[1024,1024]{1,0:T(8,128)(2,1)S(1)}, bf16[1024,1024]{1,0:T(8,128)(2,1)}, u32[]{:S(2)}) copy-start(bf16[1024,1024]{1,0:T(8,128)(2,1)} %gather_fusion.2) | copy-start | bytes 6291460
  420.2 201.5 %all-to-all-start.2 = ((bf16[128,12,1024]{2,1,0:T(8,128)(2,1)}), bf16[128,12,1024]{2,1,0:T(8,128)(2,1)}, u32[]{:S(2)}, u32[]{:S(2)}) async-start(bf16[128,12,1024]{2,1,0:T(8,128)(2,1)} %reshape.214), calls=%async_computation.2 | async-start | bytes 8388608 | tf_op jit(solution)/shard_map/all_to_all | solution.py:86
  436.4 233.7 %reduce-scatter.2.cloned.1.call-start = ((), (), s32[]{:S(2)}) async-start(), calls=%async_computation.5 | async-start | bytes 1310720 | tf_op jit(solution)/shard_map/reduce_scatter | solution.py:105
  438.7 187.7 %copy-start.10 = (s32[1536]{0:T(1024)S(1)}, s32[1536]{0:T(1024)}, u32[]{:S(2)}) copy-start(s32[1536]{0:T(1024)} %eq.67) | copy-start | bytes 18436
  626.4 1.0 copy-start.3
  626.4 1.1 copy-start.7
  626.4 1.0 copy-start.13
  626.4 1.0 copy-start.15
  626.4 1.0 copy-start.18
  626.4 1.0 copy-start.20
  635.9 7.4 %copy-start.17 = (f32[64]{0:T(128)S(1)}, f32[64]{0:T(128)}, u32[]{:S(2)}) copy-start(f32[64]{0:T(128)} %copy-done.16) | copy-start | bytes 772
Sparse Core Ops, SparseCore 0:
  11.2 152.7 all-gather.1
  643.4 26.6 reduce-scatter.1
where the time goes:
time: 680 us; the launch traced here: 679 us
  waiting for transfers between devices  496 us (73%)
  starting transfers between devices  49.2 us (7%)
  blocking collectives  48.9 us (7%)
  local copies, waits for them, and re-layouts  44.6 us (7%)
  matrix products  16.9 us (2%)
  between operations  14.4 us (2%)
  other arithmetic  8.47 us (1%)
    all_to_all x1, waiting for transfers between devices, body(): lax.all_to_all(outgoing, 'dp', split_axis=0, concat_axis=0, tiled=True)  183 us
    all_to_all x1, waiting for transfers between devices, body(): lax.all_to_all(answers, 'dp', split_axis=0, concat_axis=0, tiled=True)  183 us
    all_gather x1, waiting for transfers between devices, body(): w_cols = lax.all_gather(proj, 'dp', axis=0, tiled=True)  104 us
    reduce_scatter x1, waiting for transfers between devices, body(): lax.psum_scatter(project_back(g_emb, w_cols).astype(jnp.bfloat16), 'mp',...  25.6 us
    all_to_all x1, starting transfers between devices, body(): lax.all_to_all(requests, 'dp', split_axis=0, concat_axis=0, tiled=True)  20.4 us
    all_to_all x1, starting transfers between devices, body(): lax.all_to_all(outgoing, 'dp', split_axis=0, concat_axis=0, tiled=True)  16.2 us
  transfers between devices with their start and end apart: 5, of which 4 were waited for; matrix products, arithmetic and copies ran while one was open for 2% of the time, Pallas kernels for 0%

commit v1 on v0

v1 whole, which is shorter than its diff:
```python
import functools

import jax
import jax.numpy as jnp
from jax import lax
from jax.experimental import pallas as pl
from jax.experimental.pallas import tpu as pltpu
from jax.sharding import PartitionSpec as P

SCALE = 20.0
EPS = 1e-06
MESH = pl.DeviceIdType.MESH
F32 = jnp.float32
BF16 = jnp.bfloat16

NX, NZ, NC, NY = 4, 16, 2, 4
NDP = NX * NZ * NC
NPEER = NX * NC
HALF = NZ // 2
RUN = 4
CAP = 3
KINDS = 8


def coords():
    dp = lax.axis_index("dp")
    y = lax.axis_index("mp")
    core = lax.rem(dp, NC)
    chip = lax.div(dp, NC)
    return lax.div(chip, NZ), y, lax.rem(chip, NZ), core


def dp_index(x, z, core):
    return (x * NZ + z) * NC + core


def wrap(value, size):
    return lax.rem(value + 2 * size, size)


def remote(src, dst, send_sem, recv_sem, dp, y):
    return pltpu.make_async_remote_copy(
        src_ref=src,
        dst_ref=dst,
        send_sem=send_sem,
        recv_sem=recv_sem,
        device_id=(dp, y),
        device_id_type=MESH,
    )


def greet(peers):
    barrier = pltpu.get_barrier_semaphore()
    for dp, y in peers:
        pl.semaphore_signal(barrier, inc=1, device_id=(dp, y), device_id_type=MESH)
    pl.semaphore_wait(barrier, len(peers))


def embed_kernel(
    hq_ref, hp_ref, w_ref, emb_ref, wout_ref, hid, wbuf, y_s, y_r, x_s, x_r, z_s, z_r, c_s, c_r, o_s
):
    x, y, z, core = coords()
    me = dp_index(x, z, core)
    rows_q = hq_ref.shape[0]
    depth = w_ref.shape[0]
    width = w_ref.shape[1]
    half_w = width // 2
    right = dp_index(x, wrap(z + 1, NZ), core)
    left = dp_index(x, wrap(z - 1, NZ), core)
    sibling = dp_index(x, z, 1 - core)
    y_peers = [wrap(y + k, NY) for k in range(1, NY)]
    x_peers = [dp_index(wrap(x + k, NX), z, core) for k in range(1, NX)]
    greet(
        [(me, p) for p in y_peers] + [(p, y) for p in x_peers] + [(right, y), (left, y), (sibling, y)]
    )

    def rows_of(zb):
        return pl.ds(pl.multiple_of((zb * NC + core) * depth, depth), depth)

    def w_slice(zb, piece):
        return wbuf.at[:, rows_of(zb), pl.ds(piece * half_w, half_w)]

    wbuf[x, rows_of(z), :] = w_ref[...]
    pending = []
    x_copies = []
    for k, peer in enumerate(x_peers):
        own = wbuf.at[x, rows_of(z)]
        cp = remote(own, own, x_s.at[k], x_r.at[k], peer, y)
        cp.start()
        x_copies.append(cp)
    hid[y, 0:rows_q, :] = hq_ref[...]
    hid[y, rows_q : 2 * rows_q, :] = hp_ref[...]
    y_copies = []
    for k, peer in enumerate(y_peers):
        cp = remote(hid.at[y], hid.at[y], y_s.at[k], y_r.at[k], me, peer)
        cp.start()
        y_copies.append(cp)
    for cp in x_copies:
        cp.wait()

    def to_sibling(zb, piece, slot):
        cp = remote(
            w_slice(zb, piece), w_slice(zb, piece), c_s.at[slot, piece], c_r.at[slot, piece], sibling, y
        )
        cp.start()
        pending.append(cp)

    def ring(direction, step, piece):
        zb = wrap(z - (step - 1), NZ) if direction == 0 else wrap(z + (step - 1), NZ)
        return remote(
            w_slice(zb, piece),
            w_slice(zb, piece),
            z_s.at[direction, step - 1, piece],
            z_r.at[direction, step - 1, piece],
            right if direction == 0 else left,
            y,
        )

    live = {}
    for piece in range(2):
        for direction in range(2):
            cp = ring(direction, 1, piece)
            cp.start()
            live[direction, 1, piece] = cp
    for piece in range(2):
        to_sibling(z, piece, 0)
    for step in range(1, HALF + 1):
        for piece in range(2):
            for direction in range(2):
                if (direction, step, piece) not in live:
                    continue
                live[direction, step, piece].wait_recv()
                last = step + 1 == HALF
                if step + 1 < HALF or (last and direction == piece):
                    cp = ring(direction, step + 1, piece)
                    cp.start()
                    live[direction, step + 1, piece] = cp
                zb = wrap(z - step, NZ) if direction == 0 else wrap(z + step, NZ)
                to_sibling(zb, piece, step if direction == 0 or step == HALF else HALF + step)
    for cp in live.values():
        cp.wait_send()
    for cp in pending:
        cp.wait()
    for cp in y_copies:
        cp.wait()
    out = pltpu.make_async_copy(wbuf, wout_ref, o_s)
    out.start()
    tile = 256

    @pl.loop(0, width // tile)
    def _(t):
        cols = pl.ds(pl.multiple_of(t * tile, tile), tile)
        total = jnp.zeros((2 * rows_q, tile), F32)
        for b in range(NY):
            total = total + jnp.dot(hid[b], wbuf[b, :, cols], preferred_element_type=F32)
        emb_ref[:, cols] = total.astype(BF16)

    out.wait()


def embed(q_hidden, p_hidden, proj):
    rows = q_hidden.shape[0]
    width = q_hidden.shape[1]
    depth = proj.shape[0]
    block = depth * NDP // NX
    vmem = pl.BlockSpec(memory_space=pltpu.VMEM)
    dma = pltpu.SemaphoreType.DMA
    return pl.pallas_call(
        embed_kernel,
        out_shape=(
            jax.ShapeDtypeStruct((2 * rows, width), BF16),
            jax.ShapeDtypeStruct((NX, block, width), BF16),
        ),
        in_specs=[vmem] * 3,
        out_specs=(vmem, pl.BlockSpec(memory_space=pl.ANY)),
        scratch_shapes=[
            pltpu.VMEM((NY, 2 * rows, width), BF16),
            pltpu.VMEM((NX, block, width), BF16),
            dma((NY - 1,)),
            dma((NY - 1,)),
            dma((NX - 1,)),
            dma((NX - 1,)),
            dma((2, HALF, 2)),
            dma((2, HALF, 2)),
            dma((NZ, 2)),
            dma((NZ, 2)),
            dma,
        ],
        compiler_params=pltpu.CompilerParams(
            collective_id=0, has_side_effects=True, vmem_limit_bytes=48 * 1024 * 1024
        ),
        cost_estimate=pl.CostEstimate(
            flops=2 * 2 * rows * width * NY * width, bytes_accessed=100 * 1024 * 1024, transcendentals=0
        ),
        name="gather_embed",
    )(q_hidden, p_hidden, proj)


def nt(a, b):
    return lax.dot_general(a, b, (((1,), (1,)), ((), ())), preferred_element_type=F32)


def loss_kernel(
    emb_ref,
    w_hbm,
    sel_ref,
    idx_ref,
    part_ref,
    gq_ref,
    gp_ref,
    loss_ref,
    wbuf,
    col,
    outbox,
    recv,
    ybuf,
    dz,
    dtab,
    gpart,
    gin,
    acc,
    w_s,
    z_s,
    z_r,
    p_s,
    p_r,
    y_s,
    y_r,
    d_s,
    d_r,
    e_s,
    e_r,
    g_s,
    g_r,
):
    x, y, z, core = coords()
    me = dp_index(x, z, core)
    rank = x * NC + core
    rows2 = emb_ref.shape[0]
    rows = rows2 // 2
    width = emb_ref.shape[1]
    half_w = width // 2
    right = dp_index(x, wrap(z + 1, NZ), core)
    left = dp_index(x, wrap(z - 1, NZ), core)

    def peer_of(k):
        other = wrap(rank + k, NPEER)
        return dp_index(lax.div(other, NC), z, lax.rem(other, NC))

    y_peers = [wrap(y + k, NY) for k in range(1, NY)]
    z_peers = [dp_index(x, wrap(z + k, NZ), core) for k in range(1, NZ)]
    mates = [peer_of(k) for k in range(1, NPEER)]
    greet([(me, p) for p in y_peers] + [(p, y) for p in z_peers] + [(p, y) for p in mates])

    w_copy = pltpu.make_async_copy(w_hbm, wbuf, w_s)
    w_copy.start()
    col[0, 0:rows2, :] = emb_ref[...]

    def ring(direction, step, piece):
        src_at = piece * rows if direction == 0 or step == 1 else rows2 + piece * rows
        if step < HALF:
            src = col.at[step - 1, pl.ds(src_at, rows)]
            dst = col.at[step, pl.ds(direction * rows2 + piece * rows, rows)]
        else:
            cols = pl.ds(direction * half_w, half_w)
            src = col.at[step - 1, pl.ds(src_at, rows), cols]
            dst = col.at[0, pl.ds(rows2 + piece * rows, rows), cols]
        return remote(
            src,
            dst,
            z_s.at[direction, step - 1, piece],
            z_r.at[direction, step - 1, piece],
            right if direction == 0 else left,
            y,
        )

    live = {}
    sends = []
    for piece in range(2):
        for direction in range(2):
            live[direction, 1, piece] = ring(direction, 1, piece)
            live[direction, 1, piece].start()

    pair_rows = lax.broadcasted_iota(jnp.int32, (2 * rows2, NPEER * 2 * KINDS), 0)
    for step in range(1, HALF + 1):
        for piece in range(2):
            for direction in range(2):
                live[direction, step, piece].wait_recv()
                if step < HALF:
                    cp = ring(direction, step + 1, piece)
                    cp.start()
                    live[direction, step + 1, piece] = cp
        slot = step % HALF
        pick = (pair_rows == sel_ref[slot : slot + 1, :]).astype(F32).astype(BF16)
        rows_out = lax.dot_general(
            pick, col[slot], (((0,), (0,)), ((), ())), preferred_element_type=F32
        )
        outbox[slot] = rows_out.astype(BF16).reshape(NPEER, 2 * KINDS, width)
        for k, peer in enumerate(mates):
            cp = remote(
                outbox.at[slot, wrap(rank + k + 1, NPEER)],
                recv.at[rank, slot],
                p_s.at[slot, k],
                p_r.at[slot, k],
                peer,
                y,
            )
            cp.start()
            sends.append(cp)
        recv[rank, slot] = outbox[slot, rank]
    for cp in live.values():
        cp.wait_send()

    lane = lax.broadcasted_iota(jnp.int32, (1, rows2), 1)
    row_id = lax.broadcasted_iota(jnp.int32, (rows2, rows2), 0)
    eye = row_id == lax.broadcasted_iota(jnp.int32, (rows2, rows2), 1)
    emb = col[0, 0:rows2, :]
    pair = row_id == part_ref[0:1, :]

    def down(mask, value):
        return jnp.sum(jnp.where(mask, value, 0.0), axis=0, keepdims=True)

    def across(mask, value):
        return jnp.sum(jnp.where(mask, value, 0.0), axis=1, keepdims=True)

    def mask_of(d, r):
        return row_id == idx_ref[d, r : r + 1, :]

    gram = nt(emb, emb)
    own_sq = down(eye, gram)
    own_pos = down(pair, gram)
    for cp in sends:
        cp.wait()
    for d in range(NPEER):
        got = recv[d].reshape(rows2, width)
        cross = nt(emb, got)
        parts = [down(mask_of(d, r), cross) for r in range(RUN)]
        parts += [down(eye, nt(got, got)), own_sq, own_pos, jnp.zeros_like(own_sq)]
        ybuf[y, d] = jnp.concatenate(parts, axis=0)
    y_copies = []
    for k, peer in enumerate(y_peers):
        cp = remote(ybuf.at[y], ybuf.at[y], y_s.at[k], y_r.at[k], me, peer)
        cp.start()
        y_copies.append(cp)
    for cp in y_copies:
        cp.wait()

    sums = [((ybuf[0, d] + ybuf[1, d]) + ybuf[2, d]) + ybuf[3, d] for d in range(NPEER)]
    inv_row = 1.0 / jnp.sqrt(sums[0][5:6] + EPS)
    inv_col = across(eye, inv_row)
    pos_score = SCALE * sums[0][6:7] * inv_row * down(pair, inv_col)
    pos_exp = jnp.exp(pos_score)
    denom = across(eye, pos_exp)
    scores = []
    exps = []
    lane_inv = []
    for d in range(NPEER):
        rl = 1.0 / jnp.sqrt(sums[d][4:5] + EPS)
        lane_inv.append(rl)
        sc = []
        ex = []
        for r in range(RUN):
            mask = mask_of(d, r)
            s = SCALE * sums[d][r : r + 1] * rl * down(mask, inv_col)
            e = jnp.exp(s)
            sc.append(s)
            ex.append(e)
            denom = denom + across(mask, e)
        scores.append(sc)
        exps.append(ex)
    denom_row = down(eye, denom)
    loss_ref[...] = jnp.log(denom_row) - pos_score
    is_query = lane < rows
    dinv_row = jnp.where(is_query, 1.0 / denom_row, 0.0)
    dinv_col = across(eye, dinv_row)

    dz[0] = dinv_row
    d_copies = []
    for k, peer in enumerate(z_peers):
        cp = remote(dz.at[0], dz.at[k + 1], d_s.at[k], d_r.at[k], peer, y)
        cp.start()
        d_copies.append(cp)
    for cp in d_copies:
        cp.wait()
    e_copies = []
    for k, peer in enumerate(mates):
        cp = remote(dz, dtab.at[k + 1], e_s.at[k], e_r.at[k], peer, y)
        cp.start()
        e_copies.append(cp)
    for k in range(NZ):
        dtab[0, k] = dz[k]
    for cp in e_copies:
        cp.wait()

    place = lax.broadcasted_iota(jnp.int32, (NZ, rows2), 0)
    lane16 = lax.broadcasted_iota(jnp.int32, (NZ, rows2), 1)
    step16 = lane16 // (2 * KINDS)
    second = (lane16 // KINDS) % 2
    source = jnp.where(
        second == 0, step16, jnp.where(step16 == 0, HALF, NZ - step16)
    )
    at_source = place == source
    inner = jnp.zeros((rows2, 1), F32)
    acc[...] = jnp.zeros_like(acc)

    def add_rows(weights, values):
        high = weights.astype(BF16)
        low = (weights - high.astype(F32)).astype(BF16)
        acc[...] += jnp.dot(high, values, preferred_element_type=F32) + jnp.dot(
            low, values, preferred_element_type=F32
        )

    for d in range(NPEER):
        table = jnp.concatenate([dtab[wrap(rank - d, NPEER), k] for k in range(NZ)], axis=0)
        spread = jnp.where(row_id == idx_ref[d, 4:5, :], 1.0, 0.0)
        found = jnp.dot(table, spread, preferred_element_type=F32, precision=lax.Precision.HIGHEST)
        dl = down(at_source, found)
        weights = jnp.zeros((rows2, rows2), F32)
        for r in range(RUN):
            mask = mask_of(d, r)
            coef = SCALE * exps[d][r] * (down(mask, dinv_col) + dl)
            weights = weights + jnp.where(mask, coef * lane_inv[d], 0.0)
            inner = inner + across(mask, coef * scores[d][r] * (1.0 / SCALE))
        add_rows(weights, recv[d].reshape(rows2, width))
    pos_coef = jnp.where(is_query, SCALE * (pos_exp * dinv_row - 1.0), 0.0)
    pos_coef = pos_coef + down(pair, across(eye, pos_coef))
    add_rows(jnp.where(pair, pos_coef * inv_row, 0.0), emb)
    inner = inner + across(pair, pos_coef * pos_score * (1.0 / SCALE))
    unit = emb.astype(F32) * inv_col
    g_emb = ((acc[...] - unit * inner) * inv_col).astype(BF16)

    w_copy.wait()
    g_copies = []
    for k in range(1, NY + 1):
        block = wrap(y + k, NY)
        gpart[k - 1] = nt(g_emb, wbuf[block]).astype(BF16)
        if k < NY:
            cp = remote(gpart.at[k - 1], gin.at[k - 1], g_s.at[k - 1], g_r.at[k - 1], me, block)
            cp.start()
            g_copies.append(cp)
    total = gpart[NY - 1].astype(F32)
    for k, cp in enumerate(g_copies):
        cp.wait()
        total = total + gin[k].astype(F32)
    grads = total.astype(BF16)
    gq_ref[...] = grads[0:rows]
    gp_ref[...] = grads[rows:]


def loss_grads(emb, w_full, sel, idx, partner):
    rows2, width = emb.shape
    rows = rows2 // 2
    vmem = pl.BlockSpec(memory_space=pltpu.VMEM)
    hbm = pl.BlockSpec(memory_space=pl.ANY)
    dma = pltpu.SemaphoreType.DMA
    return pl.pallas_call(
        loss_kernel,
        out_shape=(
            jax.ShapeDtypeStruct((rows, width), BF16),
            jax.ShapeDtypeStruct((rows, width), BF16),
            jax.ShapeDtypeStruct((1, rows2), F32),
        ),
        in_specs=[vmem, hbm, vmem, vmem, vmem],
        out_specs=(vmem,) * 3,
        scratch_shapes=[
            pltpu.VMEM(w_full.shape, BF16),
            pltpu.VMEM((HALF, 2 * rows2, width), BF16),
            pltpu.VMEM((HALF, NPEER, 2 * KINDS, width), BF16),
            pltpu.VMEM((NPEER, HALF, 2 * KINDS, width), BF16),
            pltpu.VMEM((NY, NPEER, 8, rows2), F32),
            pltpu.VMEM((NZ, 1, rows2), F32),
            pltpu.VMEM((NPEER, NZ, 1, rows2), F32),
            pltpu.VMEM((NY, rows2, width), BF16),
            pltpu.VMEM((NY - 1, rows2, width), BF16),
            pltpu.VMEM((rows2, width), F32),
            dma,
            dma((2, HALF, 2)),
            dma((2, HALF, 2)),
            dma((HALF, NPEER - 1)),
            dma((HALF, NPEER - 1)),
            dma((NY - 1,)),
            dma((NY - 1,)),
            dma((NZ - 1,)),
            dma((NZ - 1,)),
            dma((NPEER - 1,)),
            dma((NPEER - 1,)),
            dma((NY - 1,)),
            dma((NY - 1,)),
        ],
        compiler_params=pltpu.CompilerParams(
            collective_id=1, has_side_effects=True, vmem_limit_bytes=48 * 1024 * 1024
        ),
        cost_estimate=pl.CostEstimate(
            flops=10**9, bytes_accessed=100 * 1024 * 1024, transcendentals=0
        ),
        name="loss_grads",
    )(emb, w_full, sel, idx, partner)


def run_tables(negatives, rows):
    runs = negatives.reshape(-1, RUN)
    count = runs.shape[0]
    owner = runs[:, 0] // rows
    local = runs % rows
    hit = owner[:, None] == jnp.arange(NDP, dtype=jnp.int32)[None, :]
    order = jnp.arange(count, dtype=jnp.int32)
    earlier = (order[:, None] > order[None, :]).astype(BF16)
    rank = jnp.dot(earlier, hit.astype(BF16), preferred_element_type=F32).astype(jnp.int32)
    query = order // (count // rows)
    picked = [
        jnp.max(jnp.where(hit, local[:, j][:, None], 0), axis=0) for j in range(RUN)
    ] + [
        jnp.max(jnp.where(hit & (rank == i), query[:, None], -1), axis=0) for i in range(CAP)
    ]
    return jnp.stack(picked, axis=0)


def body(q_hidden, p_hidden, proj, positives, negatives):
    rows = q_hidden.shape[0]
    x, y, z, core = coords()
    me = lax.axis_index("dp")
    mine = run_tables(negatives, rows)
    tables = lax.all_gather(mine, "dp", axis=0)
    emb, w_full = embed(q_hidden, p_hidden, proj)

    steps = jnp.arange(HALF, dtype=jnp.int32)
    near = jnp.stack(
        [(z - steps + NZ) % NZ, jnp.where(steps == 0, (z + HALF) % NZ, (z + steps) % NZ)], axis=1
    ).reshape(-1)
    order_z = (near[:, None] == jnp.arange(NZ, dtype=jnp.int32)[None, :]).astype(F32)

    def by_step(values):
        return jnp.round(
            jnp.einsum("...z,sz->...s", values.astype(F32), order_z, precision=lax.Precision.HIGHEST)
        ).astype(jnp.int32)

    full = tables.reshape(NX, NZ, NC, RUN + CAP, NX, NZ, NC)
    askers = lax.dynamic_index_in_dim(full, z, 1, keepdims=False)
    askers = lax.dynamic_index_in_dim(askers, x, 3, keepdims=False)
    askers = lax.dynamic_index_in_dim(askers, core, 4, keepdims=False)[:, :, :RUN]
    askers = by_step(askers).reshape(NX * NC, RUN, HALF, 2) + rows
    givers = lax.dynamic_index_in_dim(full, x, 0, keepdims=False)
    givers = lax.dynamic_index_in_dim(givers, core, 1, keepdims=False)
    givers = lax.dynamic_index_in_dim(givers, z, 3, keepdims=False)[:, RUN:]
    givers = by_step(givers.transpose(2, 3, 1, 0)).reshape(NX * NC, CAP, HALF, 2)
    unused = jnp.full((NX * NC, KINDS - RUN - CAP, HALF, 2), -1, jnp.int32)
    sel = jnp.concatenate([askers, givers, unused], axis=1)
    offset = jnp.arange(2, dtype=jnp.int32) * (2 * rows)
    sel = jnp.where(sel >= 0, sel + offset, -1)
    sel = sel.transpose(2, 0, 3, 1).reshape(HALF, NX * NC * 2 * KINDS)

    ours = mine[RUN:].reshape(CAP, NX, NZ, NC).transpose(1, 3, 0, 2)
    ours = by_step(ours)
    ours = jnp.concatenate([ours, jnp.full((NX, NC, 1, NZ), -1, jnp.int32)], axis=2)
    theirs = lax.dynamic_index_in_dim(tables, me, 2, keepdims=False)
    theirs = by_step(theirs.reshape(NX, NZ, NC, RUN + CAP).transpose(0, 2, 3, 1))
    their_p = theirs[:, :, :RUN]
    their_q = theirs[:, :, RUN:]
    p_lanes = jnp.broadcast_to(ours[..., None], (NX, NC, RUN, NZ, RUN))
    q_lanes = jnp.where(
        their_q.transpose(0, 1, 3, 2)[:, :, None] >= 0, their_p[..., None] + rows, -1
    )
    pad = jnp.full((NX, NC, RUN, NZ, KINDS - RUN - CAP), -1, jnp.int32)
    meets = jnp.concatenate([p_lanes, q_lanes, pad], axis=-1)
    asked = jnp.concatenate(
        [
            jnp.full((NX, NC, NZ, RUN), -1, jnp.int32),
            their_q.transpose(0, 1, 3, 2),
            jnp.full((NX, NC, NZ, KINDS - RUN - CAP), -1, jnp.int32),
        ],
        axis=-1,
    )[:, :, None]
    idx = jnp.concatenate([meets, asked], axis=2).reshape(NX * NC, RUN + 1, NZ * KINDS)

    local = positives % rows
    ids = jnp.arange(rows, dtype=jnp.int32)
    of_passage = jnp.sum(jnp.where(local[:, None] == ids[None, :], ids[:, None], 0), axis=0)
    partner = jnp.concatenate([local + rows, of_passage])[None, :]

    grad_q, grad_p, loss = loss_grads(emb, w_full, sel, idx, partner)
    return (grad_q, grad_p, loss[0, :rows])


def solution(mesh):
    placed = (P("dp", "mp"), P("dp", "mp"), P("dp", "mp"), P("dp"), P("dp", None))
    return jax.shard_map(
        body,
        mesh=mesh,
        in_specs=placed,
        out_specs=(P("dp", "mp"), P("dp", "mp"), P("dp")),
        check_vma=False,
    )
```

time: 680 us -> 263 us (0.39)
  waiting for transfers between devices: 496 us -> 0 us
  Pallas kernels: 0 us -> 155 us
  starting transfers between devices: 49.2 us -> 0 us
  blocking collectives: 48.9 us -> 91 us
  local copies, waits for them, and re-layouts: 44.6 us -> 12 us
  matrix products: 16.9 us -> 1.29 us
  between operations: 14.4 us -> 0.95 us
    all_to_all x3 -> x0, waiting for transfers between devices: 365 us -> none  [the longest x1 183 us: body(): lax.all_to_all(outgoing, 'dp', split_axis=0, concat_axis=0, tiled=True)]
    pallas_call x0 -> x2, Pallas kernels: none -> 155 us  [the longest x1 93.5 us: loss_grads(): pl.pallas_call(loss_kernel, out_shape=(jax.ShapeDtypeStruct((rows, width)...]
    all_gather x1 -> x0, waiting for transfers between devices: 104 us -> none  [body(): w_cols = lax.all_gather(proj, 'dp', axis=0, tiled=True)]
    all_gather x2 -> x1, blocking collectives: 22.7 us -> 91 us  [body(): tables = lax.all_gather(mine, 'dp', axis=0)]
    all_to_all x3 -> x0, starting transfers between devices: 49.2 us -> none  [the longest x1 20.4 us: body(): lax.all_to_all(requests, 'dp', split_axis=0, concat_axis=0, tiled=True)]
    psum x3 -> x0, blocking collectives: 26.2 us -> none  [the longest x1 11 us: body(): scores = SCALE * lax.psum(score_parts, 'mp')]
    reduce_scatter x1 -> x0, waiting for transfers between devices: 25.6 us -> none  [body(): lax.psum_scatter(project_back(g_emb, w_cols).astype(jnp.bfloat16), 'mp',...]
    dot_general x6 -> x5, matrix products: 16.9 us -> 1.29 us  [the longest x4 0.9 us: by_step(): jnp.einsum('...z,sz->...s', values.astype(F32), order_z, precision=lax.Pr...]
  transfers between devices with their start and end apart: 5 -> 0, of which waited for: 4 -> 0; matrix products, arithmetic and copies ran while one was open for 2% -> 0% of each run, Pallas kernels for 0% -> 0%
where the time goes in v1:
time: 263 us
  Pallas kernels  155 us (59%)
  blocking collectives  91 us (35%)
  local copies, waits for them, and re-layouts  12 us (5%)
    pallas_call x1, Pallas kernels, loss_grads(): pl.pallas_call(loss_kernel, out_shape=(jax.ShapeDtypeStruct((rows, width)...  93.5 us
    all_gather x1, blocking collectives, body(): tables = lax.all_gather(mine, 'dp', axis=0)  91 us
    pallas_call x1, Pallas kernels, embed(): pl.pallas_call(embed_kernel, out_shape=(jax.ShapeDtypeStruct((2 * rows, w...  61.7 us

profile of v1, /device:TPU:1, one launch (start us, length us, event | category | flops | bytes accessed | tf_op | source)
XLA Modules:
  0.0 262.6 jit_solution(13005397365427689733)
XLA Ops:
  0.6 0.0 copy-start.2
  0.7 0.1 pad.16.clone
  0.8 0.7 broadcast_add_fusion
  1.5 0.1 select_reduce_fusion.7
  1.6 0.1 add_bitcast_fusion.part_ref
  1.7 0.1 copy.76
  1.8 0.1 eq.88
  1.8 0.8 copy.73
  2.6 0.1 reshape.159
  2.7 0.1 add_select_fusion
  2.8 0.4 slice_reduce_fusion
  3.2 0.4 select_reduce_fusion
  3.6 0.1 stack.48
  3.7 0.1 copy.85
  3.8 0.1 stack.47
  4.0 0.1 copy.84
  4.1 0.1 stack.46
  4.2 0.1 copy.83
  4.3 0.2 fusion.3
  4.6 0.1 broadcast_in_dim.149
  4.7 91.0 %all-gather.1 = s32[128,7,128]{2,1,0:T(8,128)S(1)} all-gather(s32[1,7,128]{2,1,0:T(8,128)S(1)} %bitcast.57), channel_id=2, replica_groups=mesh['dp'=128,'mp'=4] {'dp'}, dimensions={0}, use_global_device_ids=true | all-gather | bytes 462336 | tf_op jit(solution)/shard_map/all_gather | solution.py:523
  95.7 0.4 fusion.5
  96.1 0.1 copy.87
  96.2 0.2 fusion
  96.5 0.1 copy.89
  96.7 0.1 copy.91
  96.8 0.1 add_add_fusion.2
  96.9 0.1 concatenate.30
  97.0 0.1 broadcast_select_fusion
  97.1 0.1 add_add_fusion
  97.3 0.1 concatenate.28
  97.4 5.0 %copy.74 = s32[128,7,128]{1,2,0:T(8,128)} copy(s32[128,7,128]{2,1,0:T(8,128)S(1)} %all-gather.1) | data formatting | bytes 917504 | tf_op jit(solution)/shard_map/all_gather | solution.py:523
  102.5 0.9 constant_dynamic-slice_fusion
  103.3 1.0 constant_dynamic-slice_fusion.1
  104.3 0.1 copy.79
  104.4 0.1 copy.75
  104.6 0.2 fusion.2
  104.8 0.2 fusion.4
  105.0 0.1 copy.78
  105.1 0.1 copy.99
  105.3 0.1 fusion.13
  105.4 0.1 reshape.162.sel_ref
  105.6 0.0 copy-done
  105.6 61.7 %gather_embed.1 = (bf16[128,1024]{1,0:T(8,128)(2,1)S(1)}, bf16[4,1024,1024]{2,1,0:T(8,128)(2,1)}) custom-call(bf16[64,1024]{1,0:T(8,128)(2,1)S(1)} %copy-done, bf16[64,1024]{1,0:T(8,128)(2,1)S(1)} %copy-done.1, bf16[32,1024]{1,0:T(8,128)(2,1)S(1)} %copy-done.2), custom_call_target="tpu_custom_call" | custom-call | flops 1073741824 | bytes 104857600 | tf_op jit(solution)/shard_map/gather_embed/pallas_call | solution.py:168
  167.3 93.5 %loss_grads.1 = (bf16[64,1024]{1,0:T(8,128)(2,1)S(1)}, bf16[64,1024]{1,0:T(8,128)(2,1)S(1)}, f32[1,128]{1,0:T(1,128)S(1)}) custom-call(bf16[128,1024]{1,0:T(8,128)(2,1)S(1)} %get-tuple-element.8.emb_ref, bf16[4,1024,1024]{2,1,0:T(8,128)(2,1)} %get-tuple-element.9.w_hbm, s32[8,128]{1,0:T(8,128)S(1)} %reshape.162.sel_ref, ...), custom_call_target="tpu_custom_call" | custom-call | flops 1000000000 | bytes 104857600 | tf_op jit(solution)/shard_map/loss_grads/pallas_call | solution.py:456
  260.8 0.5 slice_bitcast_fusion.1
  261.3 0.7 copy.108
  262.0 0.7 copy.109
  (21 shorter events, 0.2 us)
Async XLA Ops:
  0.6 104.9 %copy-start.2 = (bf16[32,1024]{1,0:T(8,128)(2,1)S(1)}, bf16[32,1024]{1,0:T(8,128)(2,1)}, u32[]{:S(2)}) copy-start(bf16[32,1024]{1,0:T(8,128)(2,1)} %w_ref.1) | copy-start | bytes 196612
  0.6 104.9 %copy-start.1 = (bf16[64,1024]{1,0:T(8,128)(2,1)S(1)}, bf16[64,1024]{1,0:T(8,128)(2,1)}, u32[]{:S(2)}) copy-start(bf16[64,1024]{1,0:T(8,128)(2,1)} %hp_ref.1) | copy-start | bytes 393220
  0.7 104.9 %copy-start = (bf16[64,1024]{1,0:T(8,128)(2,1)S(1)}, bf16[64,1024]{1,0:T(8,128)(2,1)}, u32[]{:S(2)}) copy-start(bf16[64,1024]{1,0:T(8,128)(2,1)} %hq_ref.1) | copy-start | bytes 393220

commit v2 on v0

v2 whole, which is shorter than its diff:
```python
import functools

import jax
import jax.numpy as jnp
from jax import lax
from jax.experimental import pallas as pl
from jax.experimental.pallas import tpu as pltpu
from jax.sharding import PartitionSpec as P

SCALE = 20.0
EPS = 1e-06
MESH = pl.DeviceIdType.MESH
F32 = jnp.float32
BF16 = jnp.bfloat16

NX, NZ, NC, NY = 4, 16, 2, 4
NDP = NX * NZ * NC
NPEER = NX * NC
HALF = NZ // 2
RUN = 4
CAP = 3
LANES = 128
XFIRST = 384
KINDS = 8


def coords():
    dp = lax.axis_index("dp")
    y = lax.axis_index("mp")
    core = lax.rem(dp, NC)
    chip = lax.div(dp, NC)
    return lax.div(chip, NZ), y, lax.rem(chip, NZ), core


def dp_index(x, z, core):
    return (x * NZ + z) * NC + core


def wrap(value, size):
    return lax.rem(value + 2 * size, size)


def remote(src, dst, send_sem, recv_sem, dp, y):
    return pltpu.make_async_remote_copy(
        src_ref=src,
        dst_ref=dst,
        send_sem=send_sem,
        recv_sem=recv_sem,
        device_id=(dp, y),
        device_id_type=MESH,
    )


def nt(a, b):
    return lax.dot_general(a, b, (((1,), (1,)), ((), ())), preferred_element_type=F32)


def mm(a, b):
    return jnp.dot(a, b, preferred_element_type=F32)


def onehot(mask):
    return jnp.where(mask, 1.0, 0.0).astype(BF16)


def iota(shape, dim):
    return lax.broadcasted_iota(jnp.int32, shape, dim)


def down(mask, value):
    return jnp.sum(jnp.where(mask, value, 0.0), axis=0, keepdims=True)


def across(mask, value):
    return jnp.sum(jnp.where(mask, value, 0.0), axis=1, keepdims=True)


def greet(peers):
    barrier = pltpu.get_barrier_semaphore()
    for dp, y in peers:
        pl.semaphore_signal(barrier, inc=1, device_id=(dp, y), device_id_type=MESH)
    pl.semaphore_wait(barrier, len(peers))


def run_table(neg_ref, rows):
    holder = iota((rows, LANES), 1)
    query = iota((rows, LANES), 0).astype(F32)
    holder = dp_index(
        lax.div(holder, NZ * NC), lax.rem(holder, NZ), lax.rem(lax.div(holder, NZ), NC)
    )
    before = onehot(iota((rows, rows), 1) < iota((rows, rows), 0))
    base = jnp.zeros((1, LANES), F32)
    passages = [base] * RUN
    queries = [base] * CAP
    for r in range(neg_ref.shape[1] // RUN):
        first = neg_ref[:, RUN * r : RUN * r + 1]
        hit = lax.div(first, rows) == holder
        rank = mm(before, onehot(hit)) + base
        base = base + jnp.sum(jnp.where(hit, 1.0, 0.0), axis=0, keepdims=True)
        for i in range(CAP):
            queries[i] = queries[i] + down(hit & (rank == float(i)), query + 1.0)
        for j in range(RUN):
            local = lax.rem(neg_ref[:, RUN * r + j : RUN * r + j + 1], rows).astype(F32)
            named = jnp.max(jnp.where(hit, local, 0.0), axis=0, keepdims=True)
            passages[j] = jnp.maximum(passages[j], named)
    return jnp.concatenate(passages + [q - 1.0 for q in queries] + [jnp.full((1, LANES), -1.0)], 0)


def seen_z(z, step, second):
    ahead = jnp.where(step == 0, HALF, step)
    return lax.rem(jnp.where(second == 0, z - step + NZ, z + ahead), NZ)


def fill_tables(tab, sel_ref, idx_ref, rank, z, rows):
    lane8 = iota((NPEER, LANES), 1)
    row8 = iota((NPEER, LANES), 0)
    row = iota((LANES, LANES), 0)
    lane = iota((LANES, LANES), 1)
    kind = lax.rem(lane8, KINDS)
    second = lax.rem(lax.div(lane8, KINDS), 2)
    group = lax.div(lane8, 2 * KINDS)
    kind_l = lax.rem(lane, KINDS)
    second_l = lax.rem(lax.div(lane, KINDS), 2)
    group_l = lax.div(lane, 2 * KINDS)

    asked = jnp.concatenate([tab[d, z] for d in range(NPEER) for _ in range(2)], axis=0).astype(BF16)
    zero8 = jnp.zeros_like(row8)
    firsts = nt(onehot(lane8 == rank * NZ + seen_z(z, row8, zero8)), asked)
    seconds = nt(onehot(lane8 == rank * NZ + seen_z(z, row8, zero8 + 1)), asked)
    from_p = jnp.where(second == 0, firsts, seconds) + float(rows)
    here = tab[rank].reshape(LANES, LANES).astype(BF16)
    spread = mm(here, onehot(row == group_l * NZ + z))
    from_q = jnp.concatenate(
        [
            down(row == seen_z(z, jnp.full_like(lane, s), second_l) * KINDS + kind_l, spread)
            for s in range(HALF)
        ],
        axis=0,
    )
    picked = jnp.where(kind < RUN, from_p, from_q)
    picked = jnp.where(picked >= 0.0, picked + (second * 2 * rows).astype(F32), -1.0)
    sel_ref[...] = picked.astype(jnp.int32)

    z_l = seen_z(z, group_l, second_l)
    by_z = onehot(lax.rem(row, NZ) == z_l)
    mine = tab[rank, z]
    me_row = onehot(lane8 == rank * NZ + z)
    about_me = jnp.concatenate(
        [
            nt(me_row, tab[d].reshape(LANES, LANES).astype(BF16))[0:1] for d in range(NPEER)
        ],
        axis=0,
    ).astype(BF16)
    wants = mm(about_me, onehot(row == z_l * KINDS + kind_l))
    for r in range(RUN):
        own = jnp.where(lax.div(lane8, NZ) == row8, mine[RUN + r : RUN + r + 1], 0.0).astype(BF16)
        theirs = mm(about_me, onehot(row == z_l * KINDS + r)) + float(rows)
        theirs = jnp.where(wants >= 0.0, theirs, -1.0)
        idx_ref[r] = jnp.where(kind < RUN, mm(own, by_z), theirs).astype(jnp.int32)
    idx_ref[RUN] = jnp.where(kind < RUN, -1.0, wants).astype(jnp.int32)


def fused_kernel(
    hq_ref,
    hp_ref,
    w_ref,
    neg_ref,
    pos_ref,
    gq_ref,
    gp_ref,
    loss_ref,
    hid,
    wbuf,
    tab,
    sel_ref,
    idx_ref,
    col,
    outbox,
    recv,
    ybuf,
    dz,
    dtab,
    gpart,
    gin,
    acc,
    h_s,
    h_r,
    t_s,
    t_r,
    u_s,
    u_r,
    a_s,
    a_r,
    b_s,
    b_r,
    ax_s,
    ax_r,
    bx_s,
    bx_r,
    bd_s,
    bd_r,
    c_s,
    c_r,
    z_s,
    z_r,
    p_s,
    p_r,
    y_s,
    y_r,
    d_s,
    d_r,
    e_s,
    e_r,
    g_s,
    g_r,
):
    x, y, z, core = coords()
    me = dp_index(x, z, core)
    rank = x * NC + core
    rows, width = hq_ref.shape
    rows2 = 2 * rows
    half_w = width // 2
    depth = w_ref.shape[0]
    right = dp_index(x, wrap(z + 1, NZ), core)
    left = dp_index(x, wrap(z - 1, NZ), core)
    x_next = dp_index(wrap(x + 1, NX), z, core)
    x_prev = dp_index(wrap(x - 1, NX), z, core)
    sibling = dp_index(x, z, 1 - core)

    def peer_of(k):
        other = wrap(rank + k, NPEER)
        return dp_index(lax.div(other, NC), z, lax.rem(other, NC))

    y_peers = [wrap(y + k, NY) for k in range(1, NY)]
    z_peers = [dp_index(x, wrap(z + k, NZ), core) for k in range(1, NZ)]
    mates = [peer_of(k) for k in range(1, NPEER)]
    greet([(me, p) for p in y_peers] + [(p, y) for p in z_peers] + [(p, y) for p in mates])

    sent = []

    def send(src, dst, send_sem, recv_sem, dp, at_y):
        cp = remote(src, dst, send_sem, recv_sem, dp, at_y)
        cp.start()
        sent.append(cp)
        return cp

    def base_of(zb):
        return pl.multiple_of((zb * NC + core) * depth, depth)

    first_cols = pl.ds(0, XFIRST)
    other_cols = pl.ds(XFIRST, width - XFIRST)

    def a_block(zb, lo, count):
        return wbuf.at[pl.ds(lo, count), pl.ds(base_of(zb), depth), first_cols]

    def b_block(xb, zb, lo=0, count=depth):
        return wbuf.at[xb, pl.ds(pl.multiple_of(base_of(zb) + lo, count), count), other_cols]

    def z_of(block):
        if block <= HALF:
            return wrap(z - block, NZ)
        return wrap(z + block - HALF, NZ)

    def a_ring(direction, step):
        zb = wrap(z - (step - 1), NZ) if direction == 0 else wrap(z + (step - 1), NZ)
        part = a_block(zb, 0, NX) if step < HALF else a_block(zb, direction * (NX // 2), NX // 2)
        to = right if direction == 0 else left
        return send(part, part, a_s.at[direction, step - 1], a_r.at[direction, step - 1], to, y)

    def b_ring(direction, step):
        zb = wrap(z - (step - 1), NZ) if direction == 0 else wrap(z + (step - 1), NZ)
        if step < HALF:
            part = b_block(x, zb)
        else:
            part = b_block(x, zb, direction * (depth // 2), depth // 2)
        to = right if direction == 0 else left
        return send(part, part, b_s.at[direction, step - 1], b_r.at[direction, step - 1], to, y)

    def b_over_x(block):
        part = b_block(x, z_of(block))
        return [
            send(part, part, bx_s.at[way, block], bx_r.at[way, block], to, y)
            for way, to in ((0, x_next), (1, x_prev))
        ]

    def b_across(block, copies):
        out = []
        for way, to in ((0, x_next), (1, x_prev)):
            copies[way].wait_recv()
            xb = wrap(x - 1, NX) if way == 0 else wrap(x + 1, NX)
            part = b_block(xb, z_of(block), way * (depth // 2), depth // 2)
            out.append(send(part, part, bd_s.at[way, block], bd_r.at[way, block], to, y))
        return out

    def to_sibling(cols, which, block):
        part = wbuf.at[:, pl.ds(base_of(z_of(block)), depth), cols]
        return send(part, part, c_s.at[which, block], c_r.at[which, block], sibling, y)

    wbuf[x, pl.ds(base_of(z), depth), :] = w_ref[...]
    own_first = wbuf.at[x, pl.ds(base_of(z), depth), first_cols]
    a_over_x = [
        send(own_first, own_first, ax_s.at[k], ax_r.at[k], dp_index(wrap(x + k + 1, NX), z, core), y)
        for k in range(NX - 1)
    ]
    b_live = {(way, 1): b_ring(way, 1) for way in range(2)}
    over_x = {0: b_over_x(0)}
    hid[y, 0:rows, :] = hq_ref[...]
    hid[y, rows:rows2, :] = hp_ref[...]
    hidden = [
        send(hid.at[y], hid.at[y], h_s.at[k], h_r.at[k], me, peer) for k, peer in enumerate(y_peers)
    ]
    for cp in a_over_x:
        cp.wait_recv()
    a_live = {(way, 1): a_ring(way, 1) for way in range(2)}
    in_chip = [to_sibling(first_cols, 0, 0)]

    tab[rank, z] = run_table(neg_ref, rows)
    over_z = [
        send(tab.at[rank, z], tab.at[rank, z], t_s.at[k], t_r.at[k], peer, y)
        for k, peer in enumerate(z_peers)
    ]
    table_x = []

    across_x = {}
    blocks_of = {0: [0]}
    for step in range(1, HALF):
        blocks_of[step] = [step, HALF + step]
    blocks_of[HALF] = [HALF]

    def finish(step):
        for block in blocks_of[step]:
            for cp in across_x[block]:
                cp.wait_recv()
            in_chip.append(to_sibling(other_cols, 1, block))

    def turn(step):
        for block in blocks_of[step]:
            across_x[block] = b_across(block, over_x[block])

    for step in range(1, HALF + 1):
        for way in range(2):
            b_live[way, step].wait_recv()
            if step < HALF:
                b_live[way, step + 1] = b_ring(way, step + 1)
                over_x[blocks_of[step][way]] = b_over_x(blocks_of[step][way])
        if step == HALF:
            over_x[HALF] = b_over_x(HALF)
        for way in range(2):
            a_live[way, step].wait_recv()
            if step < HALF:
                a_live[way, step + 1] = a_ring(way, step + 1)
                in_chip.append(to_sibling(first_cols, 0, blocks_of[step][way]))
        if step == HALF:
            in_chip.append(to_sibling(first_cols, 0, HALF))
        turn(step - 1)
        if step > 1:
            finish(step - 2)
        if step == 2:
            for cp in over_z:
                cp.wait_recv()
            table_x = [
                send(tab.at[rank], tab.at[rank], u_s.at[k], u_r.at[k], peer, y)
                for k, peer in enumerate(mates)
            ]
        if step == HALF - 2:
            for cp in table_x:
                cp.wait_recv()
            fill_tables(tab, sel_ref, idx_ref, rank, z, rows)
    turn(HALF)
    finish(HALF - 1)
    finish(HALF)
    for cp in in_chip:
        cp.wait_recv()
    for cp in hidden:
        cp.wait_recv()

    tile = 256

    @pl.loop(0, width // tile)
    def _(t):
        cols = pl.ds(pl.multiple_of(t * tile, tile), tile)
        total = jnp.zeros((rows2, tile), F32)
        for b in range(NY):
            total = total + mm(hid[b], wbuf[b, :, cols])
        col[0, 0:rows2, cols] = total.astype(BF16)

    def ring(direction, step, piece):
        src_at = piece * rows if direction == 0 or step == 1 else rows2 + piece * rows
        if step < HALF:
            src = col.at[step - 1, pl.ds(src_at, rows)]
            dst = col.at[step, pl.ds(direction * rows2 + piece * rows, rows)]
        else:
            cols = pl.ds(direction * half_w, half_w)
            src = col.at[step - 1, pl.ds(src_at, rows), cols]
            dst = col.at[0, pl.ds(rows2 + piece * rows, rows), cols]
        to = right if direction == 0 else left
        send_sem = z_s.at[direction, step - 1, piece]
        return send(src, dst, send_sem, z_r.at[direction, step - 1, piece], to, y)

    live = {}
    for piece in range(2):
        for direction in range(2):
            live[direction, 1, piece] = ring(direction, 1, piece)

    pair_rows = iota((2 * rows2, LANES), 0)
    passed = []
    for step in range(1, HALF + 1):
        for piece in range(2):
            for direction in range(2):
                live[direction, step, piece].wait_recv()
                if step < HALF:
                    live[direction, step + 1, piece] = ring(direction, step + 1, piece)
        slot = step % HALF
        pick = onehot(pair_rows == sel_ref[slot : slot + 1, :])
        picked = lax.dot_general(
            pick, col[slot], (((0,), (0,)), ((), ())), preferred_element_type=F32
        )
        outbox[slot] = picked.astype(BF16).reshape(NPEER, 2 * KINDS, width)
        for k, peer in enumerate(mates):
            src = outbox.at[slot, wrap(rank + k + 1, NPEER)]
            passed.append(
                send(src, recv.at[rank, slot], p_s.at[slot, k], p_r.at[slot, k], peer, y)
            )
        recv[rank, slot] = outbox[slot, rank]

    lane = iota((1, rows2), 1)
    row_id = iota((rows2, rows2), 0)
    lane_id = iota((rows2, rows2), 1)
    eye = row_id == lane_id
    emb = col[0, 0:rows2, :]
    local = lax.rem(pos_ref[...], rows)
    partner = jnp.concatenate([local, local], axis=1).astype(F32)
    partner_col = across(eye, partner).astype(jnp.int32)
    partner = partner.astype(jnp.int32)
    pair = ((lane_id < rows) & (row_id == partner + rows)) | (
        (row_id < rows) & (lane_id == partner_col + rows)
    )

    def mask_of(d, r):
        return row_id == idx_ref[r, d : d + 1, :]

    gram = nt(emb, emb)
    own_sq = down(eye, gram)
    own_pos = down(pair, gram)
    for cp in passed:
        cp.wait_recv()
    for d in range(NPEER):
        got = recv[d].reshape(rows2, width)
        cross = nt(emb, got)
        parts = [down(mask_of(d, r), cross) for r in range(RUN)]
        parts += [down(eye, nt(got, got)), own_sq, own_pos, jnp.zeros_like(own_sq)]
        ybuf[y, d] = jnp.concatenate(parts, axis=0)
    over_y = [
        send(ybuf.at[y], ybuf.at[y], y_s.at[k], y_r.at[k], me, peer) for k, peer in enumerate(y_peers)
    ]
    for cp in over_y:
        cp.wait_recv()

    sums = [((ybuf[0, d] + ybuf[1, d]) + ybuf[2, d]) + ybuf[3, d] for d in range(NPEER)]
    inv_row = 1.0 / jnp.sqrt(sums[0][5:6] + EPS)
    inv_col = across(eye, inv_row)
    pos_score = SCALE * sums[0][6:7] * inv_row * down(pair, inv_col)
    pos_exp = jnp.exp(pos_score)
    denom = across(eye, pos_exp)
    scores = []
    exps = []
    lane_inv = []
    for d in range(NPEER):
        rl = 1.0 / jnp.sqrt(sums[d][4:5] + EPS)
        lane_inv.append(rl)
        sc = []
        ex = []
        for r in range(RUN):
            mask = mask_of(d, r)
            s = SCALE * sums[d][r : r + 1] * rl * down(mask, inv_col)
            e = jnp.exp(s)
            sc.append(s)
            ex.append(e)
            denom = denom + across(mask, e)
        scores.append(sc)
        exps.append(ex)
    denom_row = down(eye, denom)
    loss_ref[...] = jnp.log(denom_row[:, 0:rows]) - pos_score[:, 0:rows]
    is_query = lane < rows
    dinv_row = jnp.where(is_query, 1.0 / denom_row, 0.0)
    dinv_col = across(eye, dinv_row)

    dz[0] = dinv_row
    inv_z = [
        send(dz.at[0], dz.at[k + 1], d_s.at[k], d_r.at[k], peer, y) for k, peer in enumerate(z_peers)
    ]

    pos_coef = jnp.where(is_query, SCALE * (pos_exp * dinv_row - 1.0), 0.0)
    pos_coef = pos_coef + down(pair, across(eye, pos_coef))

    def half_grads(part, dinv_at):
        rows_at = slice(part * rows, (part + 1) * rows)
        half_id = iota((rows, rows2), 0) + part * rows

        def add_rows(weights, values, fresh=False):
            high = weights.astype(BF16)
            low = (weights - high.astype(F32)).astype(BF16)
            term = mm(jnp.concatenate([high, low], axis=0), values)
            term = term[0:rows] + term[rows:]
            acc[...] = term if fresh else acc[...] + term

        half_pair = pair[rows_at]
        add_rows(jnp.where(half_pair, pos_coef * inv_row, 0.0), emb, True)
        inner = across(half_pair, pos_coef * pos_score * (1.0 / SCALE))
        for d in range(NPEER):
            weights = jnp.zeros((rows, rows2), F32)
            for r in range(RUN):
                mask = half_id == idx_ref[r, d : d + 1, :]
                coef = SCALE * exps[d][r] * dinv_at(d, r)
                weights = weights + jnp.where(mask, coef * lane_inv[d], 0.0)
                inner = inner + across(mask, coef * scores[d][r] * (1.0 / SCALE))
            add_rows(weights, recv[d].reshape(rows2, width))
        unit = emb[rows_at].astype(F32) * inv_col[rows_at]
        return ((acc[...] - unit * inner) * inv_col[rows_at]).astype(BF16)

    def project(part, g_emb):
        copies = []
        for k in range(1, NY + 1):
            block = wrap(y + k, NY)
            gpart[part, k - 1] = nt(g_emb, wbuf[block]).astype(BF16)
            if k < NY:
                mine = gpart.at[part, k - 1]
                theirs = gin.at[part, k - 1]
                copies.append(
                    send(mine, theirs, g_s.at[part, k - 1], g_r.at[part, k - 1], me, block)
                )
        return copies

    def gathered(part, copies):
        total = gpart[part, NY - 1].astype(F32)
        for k, cp in enumerate(copies):
            cp.wait_recv()
            total = total + gin[part, k].astype(F32)
        return total.astype(BF16)

    g_query = half_grads(0, lambda d, r: down(mask_of(d, r), dinv_col))
    for cp in inv_z:
        cp.wait_recv()
    inv_x = [
        send(dz, dtab.at[k + 1], e_s.at[k], e_r.at[k], peer, y) for k, peer in enumerate(mates)
    ]
    for k in range(NZ):
        dtab[0, k] = dz[k]
    q_copies = project(0, g_query)

    for cp in inv_x:
        cp.wait_recv()
    place = iota((NZ, rows2), 0)
    lane16 = iota((NZ, rows2), 1)
    step16 = lax.div(lane16, 2 * KINDS)
    second16 = lax.rem(lax.div(lane16, KINDS), 2)
    source = jnp.where(second16 == 0, step16, jnp.where(step16 == 0, HALF, NZ - step16))
    at_source = place == source
    their_inv = []
    for d in range(NPEER):
        table = jnp.concatenate([dtab[wrap(rank - d, NPEER), k] for k in range(NZ)], axis=0)
        spread = jnp.where(row_id == idx_ref[RUN, d : d + 1, :], 1.0, 0.0)
        found = jnp.dot(table, spread, preferred_element_type=F32, precision=lax.Precision.HIGHEST)
        their_inv.append(down(at_source, found))
    p_copies = project(1, half_grads(1, lambda d, r: their_inv[d]))
    gq_ref[...] = gathered(0, q_copies)
    gp_ref[...] = gathered(1, p_copies)
    for cp in sent:
        cp.wait_send()


def body(q_hidden, p_hidden, proj, positives, negatives):
    rows, width = q_hidden.shape
    rows2 = 2 * rows
    block = proj.shape[0] * NDP // NX
    vmem = pl.BlockSpec(memory_space=pltpu.VMEM)
    dma = pltpu.SemaphoreType.DMA

    def both(*shape):
        return [dma(shape), dma(shape)]

    grad_q, grad_p, loss = pl.pallas_call(
        fused_kernel,
        out_shape=(
            jax.ShapeDtypeStruct((rows, width), BF16),
            jax.ShapeDtypeStruct((rows, width), BF16),
            jax.ShapeDtypeStruct((1, rows), F32),
        ),
        in_specs=[vmem] * 5,
        out_specs=(vmem,) * 3,
        scratch_shapes=[
            pltpu.VMEM((NY, rows2, width), BF16),
            pltpu.VMEM((NX, block, width), BF16),
            pltpu.VMEM((NPEER, NZ, 8, LANES), F32),
            pltpu.VMEM((HALF, LANES), jnp.int32),
            pltpu.VMEM((RUN + 1, NPEER, LANES), jnp.int32),
            pltpu.VMEM((HALF, 2 * rows2, width), BF16),
            pltpu.VMEM((HALF, NPEER, 2 * KINDS, width), BF16),
            pltpu.VMEM((NPEER, HALF, 2 * KINDS, width), BF16),
            pltpu.VMEM((NY, NPEER, 8, rows2), F32),
            pltpu.VMEM((NZ, 1, rows2), F32),
            pltpu.VMEM((NPEER, NZ, 1, rows2), F32),
            pltpu.VMEM((2, NY, rows, width), BF16),
            pltpu.VMEM((2, NY - 1, rows, width), BF16),
            pltpu.VMEM((rows, width), F32),
        ]
        + both(NY - 1)
        + both(NZ - 1)
        + both(NPEER - 1)
        + both(2, HALF)
        + both(2, HALF)
        + both(NX - 1)
        + both(2, NZ)
        + both(2, NZ)
        + both(2, NZ)
        + both(2, HALF, 2)
        + both(HALF, NPEER - 1)
        + both(NY - 1)
        + both(NZ - 1)
        + both(NPEER - 1)
        + both(2, NY - 1),
        compiler_params=pltpu.CompilerParams(
            collective_id=0, has_side_effects=True, vmem_limit_bytes=56 * 1024 * 1024
        ),
        cost_estimate=pl.CostEstimate(
            flops=3 * 10**9, bytes_accessed=10**8, transcendentals=10**5
        ),
        name="contrastive_backward",
    )(q_hidden, p_hidden, proj, negatives, positives[None, :])
    return (grad_q, grad_p, loss[0])


def solution(mesh):
    placed = (P("dp", "mp"), P("dp", "mp"), P("dp", "mp"), P("dp"), P("dp", None))
    return jax.shard_map(
        body,
        mesh=mesh,
        in_specs=placed,
        out_specs=(P("dp", "mp"), P("dp", "mp"), P("dp")),
        check_vma=False,
    )
```

time: 680 us -> 154 us (0.23)
  waiting for transfers between devices: 496 us -> 0 us
  Pallas kernels: 0 us -> 148 us
  starting transfers between devices: 49.2 us -> 0 us
  blocking collectives: 48.9 us -> 0 us
  local copies, waits for them, and re-layouts: 44.6 us -> 4.19 us
  matrix products: 16.9 us -> 0 us
  between operations: 14.4 us -> 0.65 us
  other arithmetic: 8.47 us -> 0 us
    all_to_all x3 -> x0, waiting for transfers between devices: 365 us -> none  [the longest x1 183 us: body(): lax.all_to_all(outgoing, 'dp', split_axis=0, concat_axis=0, tiled=True)]
    pallas_call x0 -> x1, Pallas kernels: none -> 148 us  [body(): pl.pallas_call(fused_kernel, out_shape=(jax.ShapeDtypeStruct((rows, width...]
    all_gather x1 -> x0, waiting for transfers between devices: 104 us -> none  [body(): w_cols = lax.all_gather(proj, 'dp', axis=0, tiled=True)]
    all_to_all x3 -> x0, starting transfers between devices: 49.2 us -> none  [the longest x1 20.4 us: body(): lax.all_to_all(requests, 'dp', split_axis=0, concat_axis=0, tiled=True)]
    psum x3 -> x0, blocking collectives: 26.2 us -> none  [the longest x1 11 us: body(): scores = SCALE * lax.psum(score_parts, 'mp')]
    reduce_scatter x1 -> x0, waiting for transfers between devices: 25.6 us -> none  [body(): lax.psum_scatter(project_back(g_emb, w_cols).astype(jnp.bfloat16), 'mp',...]
    all_gather x2 -> x0, blocking collectives: 22.7 us -> none  [the longest x1 12 us: body(): lax.all_gather(q_hidden, 'mp', axis=1, tiled=True)]
    dot_general x6 -> x0, matrix products: 16.9 us -> none  [the longest x1 7.34 us: project_back(): lax.dot_general(grad_emb, w_cols, (((1,), (1,)), ((), ())), preferred_ele...]
  transfers between devices with their start and end apart: 5 -> 0, of which waited for: 4 -> 0; matrix products, arithmetic and copies ran while one was open for 2% -> 0% of each run, Pallas kernels for 0% -> 0%
where the time goes in v2:
time: 154 us; the launch traced here: 153 us
  Pallas kernels  148 us (96%)
  local copies, waits for them, and re-layouts  4.19 us (3%)
    pallas_call x1, Pallas kernels, body(): pl.pallas_call(fused_kernel, out_shape=(jax.ShapeDtypeStruct((rows, width...  148 us
    unnamed x8, local copies, waits for them, and re-layouts  4.19 us

profile of v2, /device:TPU:1, one launch (start us, length us, event | category | flops | bytes accessed | tf_op | source)
XLA Modules:
  0.0 153.3 jit_solution(17792380525724883508)
XLA Ops:
  0.6 1.4 copy.8.neg_ref
  2.0 148.5 %contrastive_backward.1 = (bf16[64,1024]{1,0:T(8,128)(2,1)}, bf16[64,1024]{1,0:T(8,128)(2,1)}, f32[1,64]{1,0:T(1,128)}) custom-call(bf16[64,1024]{1,0:T(8,128)(2,1)} %hq_ref.1, bf16[64,1024]{1,0:T(8,128)(2,1)} %hp_ref.1, bf16[32,1024]{1,0:T(8,128)(2,1)} %w_ref.1, s32[64,16]{1,0:T(8,128)} %copy.8.neg_ref, s32[1,64]{1,0:T(1,128)} %bitcast.2), custom_call_target="tpu_custom_call" | custom-call | flops 3000000000 | bytes 100000000 | tf_op jit(solution)/shard_map/contrastive_backward/pallas_call | solution.py:582
  150.5 0.0 copy-start
  150.5 1.6 %copy.12 = bf16[64,1024]{1,0:T(8,128)(2,1)} copy(bf16[64,1024]{1,0:T(8,128)(2,1)} %get-tuple-element.12) | data formatting | bytes 262144
  152.1 0.0 copy-done
  152.1 0.0 copy-start.1
  152.1 0.7 copy.13
  152.8 0.0 copy-done.1
  152.8 0.5 copy.14
Async XLA Ops:
  150.5 1.6 %copy-start = (bf16[64,1024]{1,0:T(8,128)(2,1)S(1)}, bf16[64,1024]{1,0:T(8,128)(2,1)}, u32[]{:S(2)}) copy-start(bf16[64,1024]{1,0:T(8,128)(2,1)} %get-tuple-element.13) | copy-start | bytes 393220
  152.1 0.7 copy-start.1

commit v3 on v2

--- a/solution.py
+++ b/solution.py
@@ -21,6 +21,8 @@
 CAP = 3
 LANES = 128
 XFIRST = 384
+APARTS = 4
+EPARTS = 4
 KINDS = 8
 
 
@@ -87,20 +89,23 @@
     query = iota((rows, LANES), 0).astype(F32)
     holder = dp_index(
         lax.div(holder, NZ * NC), lax.rem(holder, NZ), lax.rem(lax.div(holder, NZ), NC)
-    )
+    ).astype(F32)
     before = onehot(iota((rows, rows), 1) < iota((rows, rows), 0))
     base = jnp.zeros((1, LANES), F32)
     passages = [base] * RUN
     queries = [base] * CAP
-    for r in range(neg_ref.shape[1] // RUN):
-        first = neg_ref[:, RUN * r : RUN * r + 1]
-        hit = lax.div(first, rows) == holder
+    ids = neg_ref[...]
+    turn = onehot(iota((rows, rows), 0) == iota((rows, rows), 1))
+    owners = nt(turn, lax.div(ids, rows).astype(F32).astype(BF16))
+    locals_ = nt(turn, lax.rem(ids, rows).astype(F32).astype(BF16))
+    for r in range(neg_ref.shape[0] // RUN):
+        hit = owners[:, RUN * r : RUN * r + 1] == holder
         rank = mm(before, onehot(hit)) + base
         base = base + jnp.sum(jnp.where(hit, 1.0, 0.0), axis=0, keepdims=True)
         for i in range(CAP):
             queries[i] = queries[i] + down(hit & (rank == float(i)), query + 1.0)
         for j in range(RUN):
-            local = lax.rem(neg_ref[:, RUN * r + j : RUN * r + j + 1], rows).astype(F32)
+            local = locals_[:, RUN * r + j : RUN * r + j + 1]
             named = jnp.max(jnp.where(hit, local, 0.0), axis=0, keepdims=True)
             passages[j] = jnp.maximum(passages[j], named)
     return jnp.concatenate(passages + [q - 1.0 for q in queries] + [jnp.full((1, LANES), -1.0)], 0)
@@ -219,7 +224,6 @@
     rank = x * NC + core
     rows, width = hq_ref.shape
     rows2 = 2 * rows
-    half_w = width // 2
     depth = w_ref.shape[0]
     right = dp_index(x, wrap(z + 1, NZ), core)
     left = dp_index(x, wrap(z - 1, NZ), core)
@@ -234,7 +238,7 @@
     y_peers = [wrap(y + k, NY) for k in range(1, NY)]
     z_peers = [dp_index(x, wrap(z + k, NZ), core) for k in range(1, NZ)]
     mates = [peer_of(k) for k in range(1, NPEER)]
-    greet([(me, p) for p in y_peers] + [(p, y) for p in z_peers] + [(p, y) for p in mates])
+    greet([(me, p) for p in y_peers] + [(right, y), (left, y)] + [(p, y) for p in mates])
 
     sent = []
 
@@ -261,11 +265,18 @@
             return wrap(z - block, NZ)
         return wrap(z + block - HALF, NZ)
 
-    def a_ring(direction, step):
+    def a_ring(direction, step, piece):
         zb = wrap(z - (step - 1), NZ) if direction == 0 else wrap(z + (step - 1), NZ)
-        part = a_block(zb, 0, NX) if step < HALF else a_block(zb, direction * (NX // 2), NX // 2)
+        part = a_block(zb, piece * (NX // APARTS), NX // APARTS)
         to = right if direction == 0 else left
-        return send(part, part, a_s.at[direction, step - 1], a_r.at[direction, step - 1], to, y)
+        at = (direction, step - 1, piece)
+        return send(part, part, a_s.at[at], a_r.at[at], to, y)
+
+    def t_ring(direction, step):
+        zb = wrap(z - (step - 1), NZ) if direction == 0 else wrap(z + (step - 1), NZ)
+        part = tab.at[rank, zb]
+        to = right if direction == 0 else left
+        return send(part, part, t_s.at[direction, step - 1], t_r.at[direction, step - 1], to, y)
 
     def b_ring(direction, step):
         zb = wrap(z - (step - 1), NZ) if direction == 0 else wrap(z + (step - 1), NZ)
@@ -311,15 +322,14 @@
     ]
     for cp in a_over_x:
         cp.wait_recv()
-    a_live = {(way, 1): a_ring(way, 1) for way in range(2)}
+    a_live = {}
+    for piece in range(APARTS):
+        for way in range(2):
+            a_live[way, 1, piece] = a_ring(way, 1, piece)
     in_chip = [to_sibling(first_cols, 0, 0)]
 
     tab[rank, z] = run_table(neg_ref, rows)
-    over_z = [
-        send(tab.at[rank, z], tab.at[rank, z], t_s.at[k], t_r.at[k], peer, y)
-        for k, peer in enumerate(z_peers)
-    ]
-    table_x = []
+    t_live = {(way, 1): t_ring(way, 1) for way in range(2)}
 
     across_x = {}
     blocks_of = {0: [0]}
@@ -345,28 +355,32 @@
                 over_x[blocks_of[step][way]] = b_over_x(blocks_of[step][way])
         if step == HALF:
             over_x[HALF] = b_over_x(HALF)
+        for piece in range(APARTS):
+            for way in range(2):
+                if (way, step, piece) not in a_live:
+                    continue
+                a_live[way, step, piece].wait_recv()
+                if step + 1 < HALF or (step + 1 == HALF and piece * 2 // APARTS == way):
+                    a_live[way, step + 1, piece] = a_ring(way, step + 1, piece)
         for way in range(2):
-            a_live[way, step].wait_recv()
-            if step < HALF:
-                a_live[way, step + 1] = a_ring(way, step + 1)
-                in_chip.append(to_sibling(first_cols, 0, blocks_of[step][way]))
-        if step == HALF:
-            in_chip.append(to_sibling(first_cols, 0, HALF))
-        turn(step - 1)
+            if (way, step) in t_live:
+                t_live[way, step].wait_recv()
+                if step + 1 < HALF or (step + 1 == HALF and way == 0):
+                    t_live[way, step + 1] = t_ring(way, step + 1)
+        for block in blocks_of[step]:
+            in_chip.append(to_sibling(first_cols, 0, block))
         if step > 1:
-            finish(step - 2)
-        if step == 2:
-            for cp in over_z:
-                cp.wait_recv()
-            table_x = [
-                send(tab.at[rank], tab.at[rank], u_s.at[k], u_r.at[k], peer, y)
-                for k, peer in enumerate(mates)
-            ]
-        if step == HALF - 2:
-            for cp in table_x:
-                cp.wait_recv()
-            fill_tables(tab, sel_ref, idx_ref, rank, z, rows)
+            turn(step - 2)
+        if step > 3:
+            finish(step - 4)
+    table_x = [
+        send(tab.at[rank], tab.at[rank], u_s.at[k], u_r.at[k], peer, y)
+        for k, peer in enumerate(mates)
+    ]
+    turn(HALF - 1)
+    finish(HALF - 3)
     turn(HALF)
+    finish(HALF - 2)
     finish(HALF - 1)
     finish(HALF)
     for cp in in_chip:
@@ -374,41 +388,41 @@
     for cp in hidden:
         cp.wait_recv()
 
-    tile = 256
-
-    @pl.loop(0, width // tile)
-    def _(t):
-        cols = pl.ds(pl.multiple_of(t * tile, tile), tile)
+    tile = width // EPARTS
+
+    def ring(direction, step, piece):
+        src_at = 0 if direction == 0 or step == 1 else rows2
+        cols = pl.ds(piece * tile, tile)
+        src = col.at[step - 1, pl.ds(src_at, rows2), cols]
+        if step < HALF:
+            dst = col.at[step, pl.ds(direction * rows2, rows2), cols]
+        else:
+            dst = col.at[0, pl.ds(rows2, rows2), cols]
+        to = right if direction == 0 else left
+        at = (direction, step - 1, piece)
+        return send(src, dst, z_s.at[at], z_r.at[at], to, y)
+
+    live = {}
+    for piece in range(EPARTS):
         total = jnp.zeros((rows2, tile), F32)
         for b in range(NY):
-            total = total + mm(hid[b], wbuf[b, :, cols])
-        col[0, 0:rows2, cols] = total.astype(BF16)
-
-    def ring(direction, step, piece):
-        src_at = piece * rows if direction == 0 or step == 1 else rows2 + piece * rows
-        if step < HALF:
-            src = col.at[step - 1, pl.ds(src_at, rows)]
-            dst = col.at[step, pl.ds(direction * rows2 + piece * rows, rows)]
-        else:
-            cols = pl.ds(direction * half_w, half_w)
-            src = col.at[step - 1, pl.ds(src_at, rows), cols]
-            dst = col.at[0, pl.ds(rows2 + piece * rows, rows), cols]
-        to = right if direction == 0 else left
-        send_sem = z_s.at[direction, step - 1, piece]
-        return send(src, dst, send_sem, z_r.at[direction, step - 1, piece], to, y)
-
-    live = {}
-    for piece in range(2):
+            total = total + mm(hid[b], wbuf[b, :, piece * tile : (piece + 1) * tile])
+        col[0, 0:rows2, piece * tile : (piece + 1) * tile] = total.astype(BF16)
         for direction in range(2):
             live[direction, 1, piece] = ring(direction, 1, piece)
+    for cp in table_x:
+        cp.wait_recv()
+    fill_tables(tab, sel_ref, idx_ref, rank, z, rows)
 
     pair_rows = iota((2 * rows2, LANES), 0)
     passed = []
     for step in range(1, HALF + 1):
-        for piece in range(2):
+        for piece in range(EPARTS):
             for direction in range(2):
+                if (direction, step, piece) not in live:
+                    continue
                 live[direction, step, piece].wait_recv()
-                if step < HALF:
+                if step + 1 < HALF or (step + 1 == HALF and piece * 2 // EPARTS == direction):
                     live[direction, step + 1, piece] = ring(direction, step + 1, piece)
         slot = step % HALF
         pick = onehot(pair_rows == sel_ref[slot : slot + 1, :])
@@ -520,7 +534,7 @@
 
     def project(part, g_emb):
         copies = []
-        for k in range(1, NY + 1):
+        for k in (2, 1, 3, NY):
             block = wrap(y + k, NY)
             gpart[part, k - 1] = nt(g_emb, wbuf[block]).astype(BF16)
             if k < NY:
@@ -533,8 +547,9 @@
 
     def gathered(part, copies):
         total = gpart[part, NY - 1].astype(F32)
-        for k, cp in enumerate(copies):
+        for cp in copies:
             cp.wait_recv()
+        for k in range(NY - 1):
             total = total + gin[part, k].astype(F32)
         return total.astype(BF16)
 
@@ -605,15 +620,15 @@
             pltpu.VMEM((rows, width), F32),
         ]
         + both(NY - 1)
-        + both(NZ - 1)
+        + both(2, HALF)
         + both(NPEER - 1)
-        + both(2, HALF)
+        + both(2, HALF, APARTS)
         + both(2, HALF)
         + both(NX - 1)
         + both(2, NZ)
         + both(2, NZ)
         + both(2, NZ)
-        + both(2, HALF, 2)
+        + both(2, HALF, EPARTS)
         + both(HALF, NPEER - 1)
         + both(NY - 1)
         + both(NZ - 1)
@@ -626,7 +641,7 @@
             flops=3 * 10**9, bytes_accessed=10**8, transcendentals=10**5
         ),
         name="contrastive_backward",
-    )(q_hidden, p_hidden, proj, negatives, positives[None, :])
+    )(q_hidden, p_hidden, proj, negatives.T, positives[None, :])
     return (grad_q, grad_p, loss[0])
 
 

time: 154 us -> 145 us (0.942)
  Pallas kernels: 148 us -> 141 us
    pallas_call x1, Pallas kernels: 148 us -> 141 us  [body(): pl.pallas_call(fused_kernel, out_shape=(jax.ShapeDtypeStruct((rows, width...]
    unnamed x8 -> x7, local copies, waits for them, and re-layouts: 4.19 us -> 2.79 us
where the time goes in v3:
time: 145 us
  Pallas kernels  141 us (97%)
  local copies, waits for them, and re-layouts  2.79 us (2%)
    pallas_call x1, Pallas kernels, body(): pl.pallas_call(fused_kernel, out_shape=(jax.ShapeDtypeStruct((rows, width...  141 us

profile of v3, /device:TPU:1, one launch (start us, length us, event | category | flops | bytes accessed | tf_op | source)
XLA Modules:
  0.0 144.6 jit_solution(8558196970575176776)
XLA Ops:
  0.6 141.2 %contrastive_backward.1 = (bf16[64,1024]{1,0:T(8,128)(2,1)}, bf16[64,1024]{1,0:T(8,128)(2,1)}, f32[1,64]{1,0:T(1,128)}) custom-call(bf16[64,1024]{1,0:T(8,128)(2,1)} %hq_ref.1, bf16[64,1024]{1,0:T(8,128)(2,1)} %hp_ref.1, bf16[32,1024]{1,0:T(8,128)(2,1)} %w_ref.1, s32[16,64]{1,0:T(8,128)} %bitcast.3, s32[1,64]{1,0:T(1,128)} %bitcast.4), custom_call_target="tpu_custom_call" | custom-call | flops 3000000000 | bytes 100000000 | tf_op jit(solution)/shard_map/contrastive_backward/pallas_call | solution.py:597
  141.8 0.0 copy-start
  141.8 1.6 %copy.11 = bf16[64,1024]{1,0:T(8,128)(2,1)} copy(bf16[64,1024]{1,0:T(8,128)(2,1)} %get-tuple-element.12) | data formatting | bytes 262144
  143.4 0.0 copy-done
  143.4 0.0 copy-start.1
  143.4 0.7 copy.12
  144.1 0.0 copy-done.1
  144.1 0.5 copy.13
Async XLA Ops:
  141.8 1.6 %copy-start = (bf16[64,1024]{1,0:T(8,128)(2,1)S(1)}, bf16[64,1024]{1,0:T(8,128)(2,1)}, u32[]{:S(2)}) copy-start(bf16[64,1024]{1,0:T(8,128)(2,1)} %get-tuple-element.13) | copy-start | bytes 393220
  143.4 0.7 copy-start.1

commit v4 on v3

v4 whole, which is shorter than its diff:
```python
import functools

import jax
import jax.numpy as jnp
from jax import lax
from jax.experimental import pallas as pl
from jax.experimental.pallas import tpu as pltpu
from jax.sharding import PartitionSpec as P

SCALE = 20.0
EPS = 1e-06
MESH = pl.DeviceIdType.MESH
F32 = jnp.float32
BF16 = jnp.bfloat16

NX, NZ, NC, NY = 4, 16, 2, 4
NDP = NX * NZ * NC
NPEER = NX * NC
HALF = NZ // 2
RUN = 4
CAP = 3
LANES = 128
XFIRST = 384
APARTS = 4
EPARTS = 4
KINDS = 8


def coords():
    dp = lax.axis_index("dp")
    y = lax.axis_index("mp")
    core = lax.rem(dp, NC)
    chip = lax.div(dp, NC)
    return lax.div(chip, NZ), y, lax.rem(chip, NZ), core


def dp_index(x, z, core):
    return (x * NZ + z) * NC + core


def wrap(value, size):
    return lax.rem(value + 2 * size, size)


def remote(src, dst, send_sem, recv_sem, dp, y):
    return pltpu.make_async_remote_copy(
        src_ref=src,
        dst_ref=dst,
        send_sem=send_sem,
        recv_sem=recv_sem,
        device_id=(dp, y),
        device_id_type=MESH,
    )


def nt(a, b):
    return lax.dot_general(a, b, (((1,), (1,)), ((), ())), preferred_element_type=F32)


def mm(a, b):
    return jnp.dot(a, b, preferred_element_type=F32)


def onehot(mask):
    return jnp.where(mask, 1.0, 0.0).astype(BF16)


def iota(shape, dim):
    return lax.broadcasted_iota(jnp.int32, shape, dim)


def down(mask, value):
    return jnp.sum(jnp.where(mask, value, 0.0), axis=0, keepdims=True)


def across(mask, value):
    return jnp.sum(jnp.where(mask, value, 0.0), axis=1, keepdims=True)


def greet(peers):
    barrier = pltpu.get_barrier_semaphore()
    for dp, y in peers:
        pl.semaphore_signal(barrier, inc=1, device_id=(dp, y), device_id_type=MESH)
    pl.semaphore_wait(barrier, len(peers))


def run_table(neg_ref, rows):
    holder = iota((rows, LANES), 1)
    query = iota((rows, LANES), 0).astype(F32)
    holder = dp_index(
        lax.div(holder, NZ * NC), lax.rem(holder, NZ), lax.rem(lax.div(holder, NZ), NC)
    ).astype(F32)
    before = onehot(iota((rows, rows), 1) < iota((rows, rows), 0))
    base = jnp.zeros((1, LANES), F32)
    passages = [base] * RUN
    queries = [base] * CAP
    ids = neg_ref[...]
    turn = onehot(iota((rows, rows), 0) == iota((rows, rows), 1))
    owners = nt(turn, lax.div(ids, rows).astype(F32).astype(BF16))
    locals_ = nt(turn, lax.rem(ids, rows).astype(F32).astype(BF16))
    for r in range(neg_ref.shape[0] // RUN):
        hit = owners[:, RUN * r : RUN * r + 1] == holder
        rank = mm(before, onehot(hit)) + base
        base = base + jnp.sum(jnp.where(hit, 1.0, 0.0), axis=0, keepdims=True)
        for i in range(CAP):
            queries[i] = queries[i] + down(hit & (rank == float(i)), query + 1.0)
        for j in range(RUN):
            local = locals_[:, RUN * r + j : RUN * r + j + 1]
            named = jnp.max(jnp.where(hit, local, 0.0), axis=0, keepdims=True)
            passages[j] = jnp.maximum(passages[j], named)
    return jnp.concatenate(passages + [q - 1.0 for q in queries] + [jnp.full((1, LANES), -1.0)], 0)


def seen_z(z, step, second):
    ahead = jnp.where(step == 0, HALF, step)
    return lax.rem(jnp.where(second == 0, z - step + NZ, z + ahead), NZ)


def fill_picks(tab, sel_ref, rank, z, rows):
    lane8 = iota((NPEER, LANES), 1)
    row8 = iota((NPEER, LANES), 0)
    row = iota((LANES, LANES), 0)
    lane = iota((LANES, LANES), 1)
    kind = lax.rem(lane8, KINDS)
    second = lax.rem(lax.div(lane8, KINDS), 2)
    kind_l = lax.rem(lane, KINDS)
    second_l = lax.rem(lax.div(lane, KINDS), 2)
    group_l = lax.div(lane, 2 * KINDS)
    asked = jnp.concatenate([tab[d, z] for d in range(NPEER) for _ in range(2)], axis=0).astype(BF16)
    zero8 = jnp.zeros_like(row8)
    firsts = nt(onehot(lane8 == rank * NZ + seen_z(z, row8, zero8)), asked)
    seconds = nt(onehot(lane8 == rank * NZ + seen_z(z, row8, zero8 + 1)), asked)
    from_p = jnp.where(second == 0, firsts, seconds) + float(rows)
    here = tab[rank].reshape(LANES, LANES).astype(BF16)
    spread = mm(here, onehot(row == group_l * NZ + z))
    from_q = jnp.concatenate(
        [
            down(row == seen_z(z, jnp.full_like(lane, s), second_l) * KINDS + kind_l, spread)
            for s in range(HALF)
        ],
        axis=0,
    )
    picked = jnp.where(kind < RUN, from_p, from_q)
    picked = jnp.where(picked >= 0.0, picked + (second * 2 * rows).astype(F32), -1.0)
    sel_ref[...] = picked.astype(jnp.int32)


def about_this(tab, rank, z):
    lane8 = iota((NPEER, LANES), 1)
    row = iota((LANES, LANES), 0)
    lane = iota((LANES, LANES), 1)
    me_row = onehot(lane8 == rank * NZ + z)
    said = [nt(me_row, tab[d].reshape(LANES, LANES).astype(BF16))[0:1] for d in range(NPEER)]
    said = jnp.concatenate(said, axis=0)
    low = said.astype(BF16)
    first = lane - lax.rem(lane, KINDS)
    passages = [mm(low, onehot(row == first + r)) for r in range(RUN)]
    return jnp.concatenate([said] + passages, axis=0).astype(BF16)


def fill_meets(tab, about, idx_ref, step, rank, z, rows):
    row = iota((LANES, LANES), 0)
    lane = iota((LANES, LANES), 1)
    kind_l = lax.rem(lane, KINDS)
    group_l = lax.div(lane, 2 * KINDS)
    z_l = seen_z(z, jnp.full_like(lane, step), lax.rem(lax.div(lane, KINDS), 2))
    kind = kind_l[0:1]
    own = mm(tab[rank, z].astype(BF16), onehot(row == group_l * NZ + z_l))
    found = mm(about, onehot(row == z_l * KINDS + kind_l))
    from_peer = row[0:NPEER] == group_l[0:NPEER]
    picked = [down(from_peer, found[NPEER * k : NPEER * (k + 1)]) for k in range(RUN + 1)]
    wants = picked[0]
    out = []
    for r in range(RUN):
        theirs = jnp.where(wants >= 0.0, picked[1 + r] + float(rows), -1.0)
        out.append(jnp.where(kind < RUN, own[RUN + r : RUN + r + 1], theirs))
    out.append(jnp.where(kind < RUN, -1.0, wants))
    out += [jnp.full((1, LANES), -1.0)] * (8 - len(out))
    idx_ref[step] = jnp.concatenate(out, axis=0).astype(jnp.int32)


def fused_kernel(
    hq_ref,
    hp_ref,
    w_ref,
    neg_ref,
    pos_ref,
    gq_ref,
    gp_ref,
    loss_ref,
    hid,
    wbuf,
    tab,
    sel_ref,
    idx_ref,
    col,
    outbox,
    recv,
    ybuf,
    dz,
    dtab,
    gpart,
    gin,
    acc,
    h_s,
    h_r,
    t_s,
    t_r,
    u_s,
    u_r,
    a_s,
    a_r,
    b_s,
    b_r,
    ax_s,
    ax_r,
    bx_s,
    bx_r,
    bd_s,
    bd_r,
    c_s,
    c_r,
    z_s,
    z_r,
    p_s,
    p_r,
    y_s,
    y_r,
    d_s,
    d_r,
    e_s,
    e_r,
    g_s,
    g_r,
):
    x, y, z, core = coords()
    me = dp_index(x, z, core)
    rank = x * NC + core
    rows, width = hq_ref.shape
    rows2 = 2 * rows
    depth = w_ref.shape[0]
    right = dp_index(x, wrap(z + 1, NZ), core)
    left = dp_index(x, wrap(z - 1, NZ), core)
    x_next = dp_index(wrap(x + 1, NX), z, core)
    x_prev = dp_index(wrap(x - 1, NX), z, core)
    sibling = dp_index(x, z, 1 - core)

    def peer_of(k):
        other = wrap(rank + k, NPEER)
        return dp_index(lax.div(other, NC), z, lax.rem(other, NC))

    y_peers = [wrap(y + k, NY) for k in range(1, NY)]
    z_peers = [dp_index(x, wrap(z + k, NZ), core) for k in range(1, NZ)]
    mates = [peer_of(k) for k in range(1, NPEER)]
    greet([(me, p) for p in y_peers] + [(right, y), (left, y)] + [(p, y) for p in mates])

    def send(src, dst, send_sem, recv_sem, dp, at_y):
        cp = remote(src, dst, send_sem, recv_sem, dp, at_y)
        cp.start()
        return cp

    def drain(ref, sem):
        pltpu.make_async_copy(ref, ref, sem).wait()

    def base_of(zb):
        return pl.multiple_of((zb * NC + core) * depth, depth)

    first_cols = pl.ds(0, XFIRST)
    other_cols = pl.ds(XFIRST, width - XFIRST)

    def a_block(zb, lo, count):
        return wbuf.at[pl.ds(lo, count), pl.ds(base_of(zb), depth), first_cols]

    def b_block(xb, zb, lo=0, count=depth):
        return wbuf.at[xb, pl.ds(pl.multiple_of(base_of(zb) + lo, count), count), other_cols]

    def z_of(block):
        if block <= HALF:
            return wrap(z - block, NZ)
        return wrap(z + block - HALF, NZ)

    def a_ring(direction, step, piece):
        zb = wrap(z - (step - 1), NZ) if direction == 0 else wrap(z + (step - 1), NZ)
        part = a_block(zb, piece * (NX // APARTS), NX // APARTS)
        to = right if direction == 0 else left
        at = (direction, step - 1, piece)
        return send(part, part, a_s, a_r.at[at], to, y)

    def t_ring(direction, step):
        zb = wrap(z - (step - 1), NZ) if direction == 0 else wrap(z + (step - 1), NZ)
        part = tab.at[rank, zb]
        to = right if direction == 0 else left
        return send(part, part, t_s, t_r.at[direction, step - 1], to, y)

    def b_ring(direction, step):
        zb = wrap(z - (step - 1), NZ) if direction == 0 else wrap(z + (step - 1), NZ)
        if step < HALF:
            part = b_block(x, zb)
        else:
            part = b_block(x, zb, direction * (depth // 2), depth // 2)
        to = right if direction == 0 else left
        return send(part, part, b_s, b_r.at[direction, step - 1], to, y)

    def b_over_x(block):
        part = b_block(x, z_of(block))
        return [
            send(part, part, bx_s, bx_r.at[way, block], to, y)
            for way, to in ((0, x_next), (1, x_prev))
        ]

    def b_across(block, copies):
        for way, to in ((0, x_next), (1, x_prev)):
            copies[way].wait_recv()
            xb = wrap(x - 1, NX) if way == 0 else wrap(x + 1, NX)
            part = b_block(xb, z_of(block), way * (depth // 2), depth // 2)
            send(part, part, bd_s, bd_r.at[block], to, y)

    def to_sibling(cols, block):
        part = wbuf.at[:, pl.ds(base_of(z_of(block)), depth), cols]
        send(part, part, c_s, c_r, sibling, y)

    wbuf[x, pl.ds(base_of(z), depth), :] = w_ref[...]
    own_first = wbuf.at[x, pl.ds(base_of(z), depth), first_cols]
    for k in range(1, NX):
        send(own_first, own_first, ax_s, ax_r, dp_index(wrap(x + k, NX), z, core), y)
    b_live = {(way, 1): b_ring(way, 1) for way in range(2)}
    over_x = {0: b_over_x(0)}
    hid[y, 0:rows, :] = hq_ref[...]
    hid[y, rows:rows2, :] = hp_ref[...]
    for peer in y_peers:
        send(hid.at[y], hid.at[y], h_s, h_r, me, peer)
    drain(wbuf.at[0, pl.ds(0, (NX - 1) * depth), first_cols], ax_r)
    a_live = {}
    for piece in range(APARTS):
        for way in range(2):
            a_live[way, 1, piece] = a_ring(way, 1, piece)
    to_sibling(first_cols, 0)

    tab[rank, z] = run_table(neg_ref, rows)
    t_live = {(way, 1): t_ring(way, 1) for way in range(2)}

    blocks_of = {0: [0]}
    for step in range(1, HALF):
        blocks_of[step] = [step, HALF + step]
    blocks_of[HALF] = [HALF]

    def finish(step):
        for block in blocks_of[step]:
            drain(b_block(x, z), bd_r.at[block])
            to_sibling(other_cols, block)

    def turn(step):
        for block in blocks_of[step]:
            b_across(block, over_x[block])

    for turn_at in range(1, HALF + 2):
        step = turn_at
        if step <= HALF:
            for way in range(2):
                b_live[way, step].wait_recv()
                if step < HALF:
                    b_live[way, step + 1] = b_ring(way, step + 1)
                    over_x[blocks_of[step][way]] = b_over_x(blocks_of[step][way])
            if step == HALF:
                over_x[HALF] = b_over_x(HALF)
        step = turn_at - 1
        if step >= 1:
            for piece in range(APARTS):
                for way in range(2):
                    if (way, step, piece) not in a_live:
                        continue
                    a_live[way, step, piece].wait_recv()
                    if step + 1 < HALF or (step + 1 == HALF and piece * 2 // APARTS == way):
                        a_live[way, step + 1, piece] = a_ring(way, step + 1, piece)
            for way in range(2):
                if (way, step) in t_live:
                    t_live[way, step].wait_recv()
                    if step + 1 < HALF or (step + 1 == HALF and way == 0):
                        t_live[way, step + 1] = t_ring(way, step + 1)
            for block in blocks_of[step]:
                to_sibling(first_cols, block)
        if turn_at >= 2:
            turn(turn_at - 2)
        if turn_at >= 4:
            finish(turn_at - 4)
    for k, peer in enumerate(mates):
        send(tab.at[rank], tab.at[rank], u_s, u_r, peer, y)
    turn(HALF)
    for step in range(HALF - 2, HALF + 1):
        finish(step)
    drain(wbuf.at[:, pl.ds(0, NZ * depth)], c_r)
    drain(hid.at[pl.ds(0, NY - 1)], h_r)

    tile = width // EPARTS

    def ring(direction, step, piece):
        src_at = 0 if direction == 0 or step == 1 else rows2
        cols = pl.ds(piece * tile, tile)
        src = col.at[step - 1, pl.ds(src_at, rows2), cols]
        if step < HALF:
            dst = col.at[step, pl.ds(direction * rows2, rows2), cols]
        else:
            dst = col.at[0, pl.ds(rows2, rows2), cols]
        to = right if direction == 0 else left
        at = (direction, step - 1, piece)
        return send(src, dst, z_s, z_r.at[at], to, y)

    live = {}
    for piece in range(EPARTS):
        total = jnp.zeros((rows2, tile), F32)
        for b in range(NY):
            total = total + mm(hid[b], wbuf[b, :, piece * tile : (piece + 1) * tile])
        col[0, 0:rows2, piece * tile : (piece + 1) * tile] = total.astype(BF16)
        for direction in range(2):
            live[direction, 1, piece] = ring(direction, 1, piece)
    drain(tab.at[pl.ds(0, NPEER - 1)], u_r)
    fill_picks(tab, sel_ref, rank, z, rows)
    about = about_this(tab, rank, z)

    lane = iota((1, rows2), 1)
    row_id = iota((rows2, rows2), 0)
    lane_id = iota((rows2, rows2), 1)
    eye = row_id == lane_id
    emb = col[0, 0:rows2, :]
    local = lax.rem(pos_ref[...], rows)
    partner = jnp.concatenate([local, local], axis=1).astype(F32)
    partner_col = across(eye, partner).astype(jnp.int32)
    partner = partner.astype(jnp.int32)
    pair = ((lane_id < rows) & (row_id == partner + rows)) | (
        (row_id < rows) & (lane_id == partner_col + rows)
    )
    gram = nt(emb, emb)
    own_sq = down(eye, gram)
    own_pos = down(pair, gram)

    def mask_of(s, r):
        return row_id == idx_ref[s, r : r + 1, :]

    def score(s):
        fill_meets(tab, about, idx_ref, s, rank, z, rows)
        drain(recv.at[s, pl.ds(0, NPEER - 1)], p_r.at[s])
        got = recv[s].reshape(rows2, width)
        cross = nt(emb, got)
        parts = [down(mask_of(s, r), cross) for r in range(RUN)]
        parts += [down(eye, nt(got, got)), own_sq, own_pos, jnp.zeros_like(own_sq)]
        ybuf[y, s] = jnp.concatenate(parts, axis=0)

    pair_rows = iota((2 * rows2, LANES), 0)
    for step in range(1, HALF + 1):
        for piece in range(EPARTS):
            for direction in range(2):
                if (direction, step, piece) not in live:
                    continue
                live[direction, step, piece].wait_recv()
                if step + 1 < HALF or (step + 1 == HALF and piece * 2 // EPARTS == direction):
                    live[direction, step + 1, piece] = ring(direction, step + 1, piece)
        slot = step % HALF
        pick = onehot(pair_rows == sel_ref[slot : slot + 1, :])
        picked = lax.dot_general(
            pick, col[slot], (((0,), (0,)), ((), ())), preferred_element_type=F32
        )
        outbox[slot] = picked.astype(BF16).reshape(NPEER, 2 * KINDS, width)
        for k, peer in enumerate(mates):
            src = outbox.at[slot, wrap(rank + k + 1, NPEER)]
            send(src, recv.at[slot, rank], p_s, p_r.at[slot], peer, y)
        recv[slot, rank] = outbox[slot, rank]
        if step > 1:
            score(step - 1)
    score(0)

    for peer in y_peers:
        send(ybuf.at[y], ybuf.at[y], y_s, y_r, me, peer)
    drain(ybuf.at[pl.ds(0, NY - 1)], y_r)

    sums = [((ybuf[0, s] + ybuf[1, s]) + ybuf[2, s]) + ybuf[3, s] for s in range(HALF)]
    inv_row = 1.0 / jnp.sqrt(sums[0][5:6] + EPS)
    inv_col = across(eye, inv_row)
    pos_score = SCALE * sums[0][6:7] * inv_row * down(pair, inv_col)
    pos_exp = jnp.exp(pos_score)
    denom = across(eye, pos_exp)
    scores = []
    exps = []
    lane_inv = []
    for d in range(HALF):
        rl = 1.0 / jnp.sqrt(sums[d][4:5] + EPS)
        lane_inv.append(rl)
        sc = []
        ex = []
        for r in range(RUN):
            mask = mask_of(d, r)
            s = SCALE * sums[d][r : r + 1] * rl * down(mask, inv_col)
            e = jnp.exp(s)
            sc.append(s)
            ex.append(e)
            denom = denom + across(mask, e)
        scores.append(sc)
        exps.append(ex)
    denom_row = down(eye, denom)
    loss_ref[...] = jnp.log(denom_row[:, 0:rows]) - pos_score[:, 0:rows]
    is_query = lane < rows
    dinv_row = jnp.where(is_query, 1.0 / denom_row, 0.0)
    dinv_col = across(eye, dinv_row)

    dz[0] = dinv_row
    for k, peer in enumerate(z_peers):
        send(dz.at[0], dz.at[k + 1], d_s, d_r, peer, y)

    pos_coef = jnp.where(is_query, SCALE * (pos_exp * dinv_row - 1.0), 0.0)
    pos_coef = pos_coef + down(pair, across(eye, pos_coef))

    def half(part):
        return slice(part * rows, (part + 1) * rows)

    def half_weights(part, dinv_at):
        half_id = iota((rows, rows2), 0) + part * rows
        weights = []
        inners = []
        for s in range(HALF):
            weight = jnp.zeros((rows, rows2), F32)
            inner = jnp.zeros((rows, rows2), F32)
            for r in range(RUN):
                mask = half_id == idx_ref[s, r : r + 1, :]
                coef = exps[s][r] * dinv_at(s, r)
                weight = weight + jnp.where(mask, SCALE * coef * lane_inv[s], 0.0)
                inner = inner + jnp.where(mask, coef * scores[s][r], 0.0)
            weights.append(weight)
            inners.append(inner)
        return weights, inners

    def half_grads(part, weights, inner):
        def add_rows(weight, values, fresh=False):
            high = weight.astype(BF16)
            low = (weight - high.astype(F32)).astype(BF16)
            term = mm(jnp.concatenate([high, low], axis=0), values)
            term = term[0:rows] + term[rows:]
            acc[...] = term if fresh else acc[...] + term

        half_pair = pair[half(part)]
        add_rows(jnp.where(half_pair, pos_coef * inv_row, 0.0), emb, True)
        inner = jnp.sum(inner, axis=1, keepdims=True)
        inner = inner + across(half_pair, pos_coef * pos_score * (1.0 / SCALE))
        for s in range(HALF):
            add_rows(weights[s], recv[s].reshape(rows2, width))
        unit = emb[half(part)].astype(F32) * inv_col[half(part)]
        return ((acc[...] - unit * inner) * inv_col[half(part)]).astype(BF16)

    def project(part, g_emb):
        for k in (2, 1, 3, NY):
            block = wrap(y + k, NY)
            gpart[part, k - 1] = nt(g_emb, wbuf[block]).astype(BF16)
            if k < NY:
                mine = gpart.at[part, k - 1]
                theirs = gin.at[part, k - 1]
                send(mine, theirs, g_s, g_r.at[part], me, block)

    def gathered(part):
        total = gpart[part, NY - 1].astype(F32)
        drain(gin.at[part], g_r.at[part])
        for k in range(NY - 1):
            total = total + gin[part, k].astype(F32)
        return total.astype(BF16)

    weights, inners = half_weights(0, lambda s, r: down(mask_of(s, r), dinv_col))
    g_query = half_grads(0, weights, sum(inners))
    drain(dz.at[pl.ds(0, NZ - 1)], d_r)
    for k, peer in enumerate(mates):
        send(dz, dtab.at[k + 1], e_s, e_r, peer, y)
    for k in range(NZ):
        dtab[0, k] = dz[k]
    project(0, g_query)

    weights, inners = half_weights(1, lambda s, r: 1.0)
    drain(dtab.at[pl.ds(0, NPEER - 1)], e_r)
    at_source = iota((NZ, rows2), 0) == lax.div(iota((NZ, rows2), 1), KINDS)
    inner = jnp.zeros((rows, rows2), F32)
    for s in range(HALF):
        ahead = (s, NZ - s) if s else (0, HALF)
        table = [dtab[wrap(rank - d, NPEER), k] for d in range(NPEER) for k in ahead]
        table = jnp.concatenate(table, axis=0)
        spread = jnp.where(row_id == idx_ref[s, RUN : RUN + 1, :], 1.0, 0.0)
        found = jnp.dot(table, spread, preferred_element_type=F32, precision=lax.Precision.HIGHEST)
        their_inv = down(at_source, found)
        weights[s] = weights[s] * their_inv
        inner = inner + inners[s] * their_inv
    project(1, half_grads(1, weights, inner))
    gq_ref[...] = gathered(0)
    gp_ref[...] = gathered(1)

    drain(hid.at[pl.ds(0, NY - 1)], h_s)
    drain(tab.at[0, pl.ds(0, NZ - 1)], t_s)
    drain(tab.at[pl.ds(0, NPEER - 1)], u_s)
    drain(wbuf.at[:, pl.ds(0, (NZ - 1) * depth), first_cols], a_s)
    drain(wbuf.at[0, pl.ds(0, (NZ - 1) * depth), other_cols], b_s)
    drain(wbuf.at[0, pl.ds(0, (NX - 1) * depth), first_cols], ax_s)
    drain(wbuf.at[0, pl.ds(0, 2 * NZ * depth), other_cols], bx_s)
    drain(wbuf.at[0, pl.ds(0, NZ * depth), other_cols], bd_s)
    drain(wbuf.at[:, pl.ds(0, NZ * depth)], c_s)
    drain(col.at[:, pl.ds(0, rows2 * (NZ - 1) // HALF)], z_s)
    drain(outbox.at[:, pl.ds(0, NPEER - 1)], p_s)
    drain(ybuf.at[pl.ds(0, NY - 1)], y_s)
    drain(dz.at[pl.ds(0, NZ - 1)], d_s)
    drain(dtab.at[pl.ds(0, NPEER - 1)], e_s)
    drain(gin, g_s)


def body(q_hidden, p_hidden, proj, positives, negatives):
    rows, width = q_hidden.shape
    rows2 = 2 * rows
    block = proj.shape[0] * NDP // NX
    vmem = pl.BlockSpec(memory_space=pltpu.VMEM)
    dma = pltpu.SemaphoreType.DMA

    grad_q, grad_p, loss = pl.pallas_call(
        fused_kernel,
        out_shape=(
            jax.ShapeDtypeStruct((rows, width), BF16),
            jax.ShapeDtypeStruct((rows, width), BF16),
            jax.ShapeDtypeStruct((1, rows), F32),
        ),
        in_specs=[vmem] * 5,
        out_specs=(vmem,) * 3,
        scratch_shapes=[
            pltpu.VMEM((NY, rows2, width), BF16),
            pltpu.VMEM((NX, block, width), BF16),
            pltpu.VMEM((NPEER, NZ, 8, LANES), F32),
            pltpu.VMEM((HALF, LANES), jnp.int32),
            pltpu.VMEM((HALF, 8, LANES), jnp.int32),
            pltpu.VMEM((HALF, 2 * rows2, width), BF16),
            pltpu.VMEM((HALF, NPEER, 2 * KINDS, width), BF16),
            pltpu.VMEM((HALF, NPEER, 2 * KINDS, width), BF16),
            pltpu.VMEM((NY, NPEER, 8, rows2), F32),
            pltpu.VMEM((NZ, 1, rows2), F32),
            pltpu.VMEM((NPEER, NZ, 1, rows2), F32),
            pltpu.VMEM((2, NY, rows, width), BF16),
            pltpu.VMEM((2, NY - 1, rows, width), BF16),
            pltpu.VMEM((rows, width), F32),
        ]
        + [dma, dma]
        + [dma, dma((2, HALF))]
        + [dma, dma]
        + [dma, dma((2, HALF, APARTS))]
        + [dma, dma((2, HALF))]
        + [dma, dma]
        + [dma, dma((2, NZ))]
        + [dma, dma((NZ,))]
        + [dma, dma]
        + [dma, dma((2, HALF, EPARTS))]
        + [dma, dma((HALF,))]
        + [dma, dma]
        + [dma, dma]
        + [dma, dma]
        + [dma, dma((2,))],
        compiler_params=pltpu.CompilerParams(
            collective_id=0, has_side_effects=True, vmem_limit_bytes=56 * 1024 * 1024
        ),
        cost_estimate=pl.CostEstimate(
            flops=3 * 10**9, bytes_accessed=10**8, transcendentals=10**5
        ),
        name="contrastive_backward",
    )(q_hidden, p_hidden, proj, negatives.T, positives[None, :])
    return (grad_q, grad_p, loss[0])


def solution(mesh):
    placed = (P("dp", "mp"), P("dp", "mp"), P("dp", "mp"), P("dp"), P("dp", None))
    return jax.shard_map(
        body,
        mesh=mesh,
        in_specs=placed,
        out_specs=(P("dp", "mp"), P("dp", "mp"), P("dp")),
        check_vma=False,
    )
```

time: 145 us -> 140 us (0.966)
  Pallas kernels: 141 us -> 137 us
    pallas_call x1, Pallas kernels: 141 us -> 137 us  [body(): pl.pallas_call(fused_kernel, out_shape=(jax.ShapeDtypeStruct((rows, width...]
where the time goes in v4:
time: 140 us
  Pallas kernels  137 us (98%)
  local copies, waits for them, and re-layouts  2.79 us (2%)
    pallas_call x1, Pallas kernels, body(): pl.pallas_call(fused_kernel, out_shape=(jax.ShapeDtypeStruct((rows, width...  137 us

profile of v4, /device:TPU:1, one launch (start us, length us, event | category | flops | bytes accessed | tf_op | source)
XLA Modules:
  0.0 140.3 jit_solution(8949624340824413403)
XLA Ops:
  0.6 136.9 %contrastive_backward.1 = (bf16[64,1024]{1,0:T(8,128)(2,1)}, bf16[64,1024]{1,0:T(8,128)(2,1)}, f32[1,64]{1,0:T(1,128)}) custom-call(bf16[64,1024]{1,0:T(8,128)(2,1)} %hq_ref.1, bf16[64,1024]{1,0:T(8,128)(2,1)} %hp_ref.1, bf16[32,1024]{1,0:T(8,128)(2,1)} %w_ref.1, s32[16,64]{1,0:T(8,128)} %bitcast.3, s32[1,64]{1,0:T(1,128)} %bitcast.4), custom_call_target="tpu_custom_call" | custom-call | flops 3000000000 | bytes 100000000 | tf_op jit(solution)/shard_map/contrastive_backward/pallas_call | solution.py:613
  137.5 0.0 copy-start
  137.5 1.6 %copy.11 = bf16[64,1024]{1,0:T(8,128)(2,1)} copy(bf16[64,1024]{1,0:T(8,128)(2,1)} %get-tuple-element.12) | data formatting | bytes 262144
  139.1 0.0 copy-done
  139.1 0.0 copy-start.1
  139.1 0.7 copy.12
  139.8 0.0 copy-done.1
  139.8 0.5 copy.13
Async XLA Ops:
  137.5 1.6 %copy-start = (bf16[64,1024]{1,0:T(8,128)(2,1)S(1)}, bf16[64,1024]{1,0:T(8,128)(2,1)}, u32[]{:S(2)}) copy-start(bf16[64,1024]{1,0:T(8,128)(2,1)} %get-tuple-element.13) | copy-start | bytes 393220
  139.1 0.7 copy-start.1

commit v5 on v4

--- a/solution.py
+++ b/solution.py
@@ -20,7 +20,7 @@
 RUN = 4
 CAP = 3
 LANES = 128
-XFIRST = 384
+XFIRST = 256
 APARTS = 4
 EPARTS = 4
 KINDS = 8
@@ -379,14 +379,12 @@
                         t_live[way, step + 1] = t_ring(way, step + 1)
             for block in blocks_of[step]:
                 to_sibling(first_cols, block)
-        if turn_at >= 2:
-            turn(turn_at - 2)
-        if turn_at >= 4:
-            finish(turn_at - 4)
+        turn(turn_at - 1)
+        if turn_at >= 3:
+            finish(turn_at - 3)
     for k, peer in enumerate(mates):
         send(tab.at[rank], tab.at[rank], u_s, u_r, peer, y)
-    turn(HALF)
-    for step in range(HALF - 2, HALF + 1):
+    for step in range(HALF - 1, HALF + 1):
         finish(step)
     drain(wbuf.at[:, pl.ds(0, NZ * depth)], c_r)
     drain(hid.at[pl.ds(0, NY - 1)], h_r)
@@ -528,19 +526,19 @@
         return weights, inners
 
     def half_grads(part, weights, inner):
-        def add_rows(weight, values, fresh=False):
+        def weighted(weight, values):
             high = weight.astype(BF16)
             low = (weight - high.astype(F32)).astype(BF16)
             term = mm(jnp.concatenate([high, low], axis=0), values)
-            term = term[0:rows] + term[rows:]
-            acc[...] = term if fresh else acc[...] + term
+            return term[0:rows] + term[rows:]
 
         half_pair = pair[half(part)]
-        add_rows(jnp.where(half_pair, pos_coef * inv_row, 0.0), emb, True)
         inner = jnp.sum(inner, axis=1, keepdims=True)
         inner = inner + across(half_pair, pos_coef * pos_score * (1.0 / SCALE))
-        for s in range(HALF):
-            add_rows(weights[s], recv[s].reshape(rows2, width))
+        arrived = recv[...].reshape(HALF * rows2, width)
+        acc[...] = weighted(jnp.where(half_pair, pos_coef * inv_row, 0.0), emb) + weighted(
+            jnp.concatenate(weights, axis=1), arrived
+        )
         unit = emb[half(part)].astype(F32) * inv_col[half(part)]
         return ((acc[...] - unit * inner) * inv_col[half(part)]).astype(BF16)
 
@@ -577,8 +575,13 @@
         ahead = (s, NZ - s) if s else (0, HALF)
         table = [dtab[wrap(rank - d, NPEER), k] for d in range(NPEER) for k in ahead]
         table = jnp.concatenate(table, axis=0)
-        spread = jnp.where(row_id == idx_ref[s, RUN : RUN + 1, :], 1.0, 0.0)
-        found = jnp.dot(table, spread, preferred_element_type=F32, precision=lax.Precision.HIGHEST)
+        high = table.astype(BF16)
+        rest = table - high.astype(F32)
+        middle = rest.astype(BF16)
+        low = (rest - middle.astype(F32)).astype(BF16)
+        spread = onehot(row_id == idx_ref[s, RUN : RUN + 1, :])
+        found = mm(jnp.concatenate([high, middle, low], axis=0), spread)
+        found = (found[0:NZ] + found[NZ : 2 * NZ]) + found[2 * NZ :]
         their_inv = down(at_source, found)
         weights[s] = weights[s] * their_inv
         inner = inner + inners[s] * their_inv

time: 140 us -> 137 us (0.979)
  Pallas kernels: 137 us -> 134 us
    pallas_call x1, Pallas kernels: 137 us -> 134 us  [body(): pl.pallas_call(fused_kernel, out_shape=(jax.ShapeDtypeStruct((rows, width...]
where the time goes in v5:
time: 137 us
  Pallas kernels  134 us (98%)
  local copies, waits for them, and re-layouts  2.79 us (2%)
    pallas_call x1, Pallas kernels, body(): pl.pallas_call(fused_kernel, out_shape=(jax.ShapeDtypeStruct((rows, width...  134 us
    unnamed x7, local copies, waits for them, and re-layouts  2.79 us

profile of v5, /device:TPU:1, one launch (start us, length us, event | category | flops | bytes accessed | tf_op | source)
XLA Modules:
  0.0 137.2 jit_solution(4212055322991221784)
XLA Ops:
  0.6 133.7 %contrastive_backward.1 = (bf16[64,1024]{1,0:T(8,128)(2,1)}, bf16[64,1024]{1,0:T(8,128)(2,1)}, f32[1,64]{1,0:T(1,128)}) custom-call(bf16[64,1024]{1,0:T(8,128)(2,1)} %hq_ref.1, bf16[64,1024]{1,0:T(8,128)(2,1)} %hp_ref.1, bf16[32,1024]{1,0:T(8,128)(2,1)} %w_ref.1, s32[16,64]{1,0:T(8,128)} %bitcast.3, s32[1,64]{1,0:T(1,128)} %bitcast.4), custom_call_target="tpu_custom_call" | custom-call | flops 3000000000 | bytes 100000000 | tf_op jit(solution)/shard_map/contrastive_backward/pallas_call | solution.py:616
  134.4 0.0 copy-start
  134.4 1.6 %copy.11 = bf16[64,1024]{1,0:T(8,128)(2,1)} copy(bf16[64,1024]{1,0:T(8,128)(2,1)} %get-tuple-element.12) | data formatting | bytes 262144
  136.0 0.0 copy-done
  136.0 0.0 copy-start.1
  136.0 0.7 copy.12
  136.6 0.0 copy-done.1
  136.7 0.5 copy.13
Async XLA Ops:
  134.4 1.6 %copy-start = (bf16[64,1024]{1,0:T(8,128)(2,1)S(1)}, bf16[64,1024]{1,0:T(8,128)(2,1)}, u32[]{:S(2)}) copy-start(bf16[64,1024]{1,0:T(8,128)(2,1)} %get-tuple-element.13) | copy-start | bytes 393220
  136.0 0.7 copy-start.1

commit v6 on v5

--- a/solution.py
+++ b/solution.py
@@ -411,10 +411,6 @@
         col[0, 0:rows2, piece * tile : (piece + 1) * tile] = total.astype(BF16)
         for direction in range(2):
             live[direction, 1, piece] = ring(direction, 1, piece)
-    drain(tab.at[pl.ds(0, NPEER - 1)], u_r)
-    fill_picks(tab, sel_ref, rank, z, rows)
-    about = about_this(tab, rank, z)
-
     lane = iota((1, rows2), 1)
     row_id = iota((rows2, rows2), 0)
     lane_id = iota((rows2, rows2), 1)
@@ -427,9 +423,6 @@
     pair = ((lane_id < rows) & (row_id == partner + rows)) | (
         (row_id < rows) & (lane_id == partner_col + rows)
     )
-    gram = nt(emb, emb)
-    own_sq = down(eye, gram)
-    own_pos = down(pair, gram)
 
     def mask_of(s, r):
         return row_id == idx_ref[s, r : r + 1, :]
@@ -452,6 +445,13 @@
                 live[direction, step, piece].wait_recv()
                 if step + 1 < HALF or (step + 1 == HALF and piece * 2 // EPARTS == direction):
                     live[direction, step + 1, piece] = ring(direction, step + 1, piece)
+        if step == 1:
+            drain(tab.at[pl.ds(0, NPEER - 1)], u_r)
+            fill_picks(tab, sel_ref, rank, z, rows)
+            about = about_this(tab, rank, z)
+            gram = nt(emb, emb)
+            own_sq = down(eye, gram)
+            own_pos = down(pair, gram)
         slot = step % HALF
         pick = onehot(pair_rows == sel_ref[slot : slot + 1, :])
         picked = lax.dot_general(
@@ -560,6 +560,7 @@
 
     weights, inners = half_weights(0, lambda s, r: down(mask_of(s, r), dinv_col))
     g_query = half_grads(0, weights, sum(inners))
+    weights, inners = half_weights(1, lambda s, r: 1.0)
     drain(dz.at[pl.ds(0, NZ - 1)], d_r)
     for k, peer in enumerate(mates):
         send(dz, dtab.at[k + 1], e_s, e_r, peer, y)
@@ -567,7 +568,6 @@
         dtab[0, k] = dz[k]
     project(0, g_query)
 
-    weights, inners = half_weights(1, lambda s, r: 1.0)
     drain(dtab.at[pl.ds(0, NPEER - 1)], e_r)
     at_source = iota((NZ, rows2), 0) == lax.div(iota((NZ, rows2), 1), KINDS)
     inner = jnp.zeros((rows, rows2), F32)

time: 137 us -> 137 us (level)
  no operation moved by 1% of the time
where the time goes in v6:
time: 137 us
  Pallas kernels  134 us (98%)
  local copies, waits for them, and re-layouts  2.79 us (2%)
    pallas_call x1, Pallas kernels, body(): pl.pallas_call(fused_kernel, out_shape=(jax.ShapeDtypeStruct((rows, width...  134 us
    unnamed x7, local copies, waits for them, and re-layouts  2.79 us

profile of v6, /device:TPU:1, one launch (start us, length us, event | category | flops | bytes accessed | tf_op | source)
XLA Modules:
  0.0 137.2 jit_solution(10860345105512184359)
XLA Ops:
  0.6 133.7 %contrastive_backward.1 = (bf16[64,1024]{1,0:T(8,128)(2,1)}, bf16[64,1024]{1,0:T(8,128)(2,1)}, f32[1,64]{1,0:T(1,128)}) custom-call(bf16[64,1024]{1,0:T(8,128)(2,1)} %hq_ref.1, bf16[64,1024]{1,0:T(8,128)(2,1)} %hp_ref.1, bf16[32,1024]{1,0:T(8,128)(2,1)} %w_ref.1, s32[16,64]{1,0:T(8,128)} %bitcast.3, s32[1,64]{1,0:T(1,128)} %bitcast.4), custom_call_target="tpu_custom_call" | custom-call | flops 3000000000 | bytes 100000000 | tf_op jit(solution)/shard_map/contrastive_backward/pallas_call | solution.py:616
  134.4 0.0 copy-start
  134.4 1.6 %copy.11 = bf16[64,1024]{1,0:T(8,128)(2,1)} copy(bf16[64,1024]{1,0:T(8,128)(2,1)} %get-tuple-element.12) | data formatting | bytes 262144
  136.0 0.0 copy-done
  136.0 0.0 copy-start.1
  136.0 0.7 copy.12
  136.6 0.0 copy-done.1
  136.6 0.5 copy.13
Async XLA Ops:
  134.4 1.6 %copy-start = (bf16[64,1024]{1,0:T(8,128)(2,1)S(1)}, bf16[64,1024]{1,0:T(8,128)(2,1)}, u32[]{:S(2)}) copy-start(bf16[64,1024]{1,0:T(8,128)(2,1)} %get-tuple-element.13) | copy-start | bytes 393220
  136.0 0.7 copy-start.1

commit v7 on v5

--- a/solution.py
+++ b/solution.py
@@ -464,10 +464,13 @@
         recv[slot, rank] = outbox[slot, rank]
         if step > 1:
             score(step - 1)
+    most = ybuf.at[y, pl.ds(1, HALF - 1)]
+    for peer in y_peers:
+        send(most, most, y_s, y_r, me, peer)
     score(0)
 
     for peer in y_peers:
-        send(ybuf.at[y], ybuf.at[y], y_s, y_r, me, peer)
+        send(ybuf.at[y, 0], ybuf.at[y, 0], y_s, y_r, me, peer)
     drain(ybuf.at[pl.ds(0, NY - 1)], y_r)
 
     sums = [((ybuf[0, s] + ybuf[1, s]) + ybuf[2, s]) + ybuf[3, s] for s in range(HALF)]

time: 137 us -> 137 us (level)
  no operation moved by 1% of the time
where the time goes in v7:
time: 137 us; the launch traced here: 136 us
  Pallas kernels  133 us (97%)
  local copies, waits for them, and re-layouts  2.79 us (2%)
    pallas_call x1, Pallas kernels, body(): pl.pallas_call(fused_kernel, out_shape=(jax.ShapeDtypeStruct((rows, width...  133 us
    unnamed x7, local copies, waits for them, and re-layouts  2.79 us

profile of v7, /device:TPU:1, one launch (start us, length us, event | category | flops | bytes accessed | tf_op | source)
XLA Modules:
  0.0 136.4 jit_solution(8793198210615562491)
XLA Ops:
  0.6 133.0 %contrastive_backward.1 = (bf16[64,1024]{1,0:T(8,128)(2,1)}, bf16[64,1024]{1,0:T(8,128)(2,1)}, f32[1,64]{1,0:T(1,128)}) custom-call(bf16[64,1024]{1,0:T(8,128)(2,1)} %hq_ref.1, bf16[64,1024]{1,0:T(8,128)(2,1)} %hp_ref.1, bf16[32,1024]{1,0:T(8,128)(2,1)} %w_ref.1, s32[16,64]{1,0:T(8,128)} %bitcast.3, s32[1,64]{1,0:T(1,128)} %bitcast.4), custom_call_target="tpu_custom_call" | custom-call | flops 3000000000 | bytes 100000000 | tf_op jit(solution)/shard_map/contrastive_backward/pallas_call | solution.py:619
  133.6 0.0 copy-start
  133.7 1.6 %copy.11 = bf16[64,1024]{1,0:T(8,128)(2,1)} copy(bf16[64,1024]{1,0:T(8,128)(2,1)} %get-tuple-element.12) | data formatting | bytes 262144
  135.3 0.0 copy-done
  135.3 0.0 copy-start.1
  135.3 0.7 copy.12
  135.9 0.0 copy-done.1
  135.9 0.5 copy.13
Async XLA Ops:
  133.6 1.6 %copy-start = (bf16[64,1024]{1,0:T(8,128)(2,1)S(1)}, bf16[64,1024]{1,0:T(8,128)(2,1)}, u32[]{:S(2)}) copy-start(bf16[64,1024]{1,0:T(8,128)(2,1)} %get-tuple-element.13) | copy-start | bytes 393220
  135.3 0.7 copy-start.1
